TPU v7x, 256 devices: a whole 4x4x8 slice. The times are simulated.
256 devices in a mesh: gx: 16 (over z, y_hi), gy: 16 (over y_lo, x, core).
Axes of the slice: x: 4, y: 4 (y_hi: 2, y_lo: 2; y = y_hi * 2 + y_lo), z: 8, core: 2. Of those that a mesh axis runs over, the one named last changes fastest.
Arguments:
- populations: float32 [19, 64, 128, 128], P(None, 'gx', 'gy'), may hold values from 0.02 to 0.1
- flags: int32 [64, 128, 128], P('gx', 'gy'), may hold values from 0 to 1, as said below
- block_tile: int32 [4096, 1], P(('gx', 'gy')), may hold values from 0 to 15; in each aligned block of 16 rows (0 to 15, 16 to 31, ...) at most 2 rows name the same one
- marker_cell: int32 [4096, 128], P(('gx', 'gy')), may hold values from 1 to 2941, as said below
- marker_frac: float32 [4096, 3, 128], P(('gx', 'gy')), may hold values from 0 to 1
- marker_live: int32 [4096, 128], P(('gx', 'gy')), may hold values 0 or 1
- marker_target: float32 [4096, 3, 128], P(('gx', 'gy')), may hold values from -0.3 to 0.3
- marker_force: float32 [4096, 3, 128], P(('gx', 'gy')), may hold values from -0.3 to 0.3
Outputs:
- populations_out: float32 [19, 64, 128, 128], P(None, 'gx', 'gy')
- marker_force_out: float32 [4096, 3, 128], P(('gx', 'gy'))
Inputs may be any that keep to these rules, and one draw needn't show every extreme that they name: `flags`: every cell of the first and of the last layer along z is a wall. `block_tile`: A block's tile lies in its owner's gy column; among the 16 rows of one device at most 2 name the same tile. `marker_cell`: equal to (i * 8 + j) * 128 + k with i < 3, j < 7 and 1 <= k < 126, so a marker's box lies inside its tile.
All inputs are finite; a program needn't handle non-finite values. No bound on the sum of `marker_live` on one device may be relied on, other than what follows from the above.
Results may differ from a plain program's by a relative error of at most 0.0001.
Values sent between devices are 32-bit elements; how exact they have to be, the bound alone decides.
A program may use at most 64 MiB of HBM per device.

v0:
```python
import jax
import jax.numpy as jnp
from jax import lax
from jax.sharding import PartitionSpec as P

STEPS = 2
SLOT = 2


VELOCITIES = (
    (0, 0, 0),
    (1, 0, 0),
    (-1, 0, 0),
    (0, 1, 0),
    (0, -1, 0),
    (0, 0, 1),
    (0, 0, -1),
    (1, 1, 0),
    (-1, -1, 0),
    (1, -1, 0),
    (-1, 1, 0),
    (1, 0, 1),
    (-1, 0, -1),
    (1, 0, -1),
    (-1, 0, 1),
    (0, 1, 1),
    (0, -1, -1),
    (0, 1, -1),
    (0, -1, 1),
)
OPPOSITE = (0, 2, 1, 4, 3, 6, 5, 8, 7, 10, 9, 12, 11, 14, 13, 16, 15, 18, 17)
WEIGHTS = (1.0 / 3.0,) + (1.0 / 18.0,) * 6 + (1.0 / 36.0,) * 12
OMEGA = 1.25
HIGHEST = lax.Precision.HIGHEST


def with_halo(block, sides, width):
    for axis, dim in sides:
        count = lax.axis_size(axis)
        forward = [(i, i + 1) for i in range(count - 1)]
        forward.append((count - 1, 0))
        backward = [(target, source) for source, target in forward]
        low = lax.ppermute(
            lax.slice_in_dim(block, block.shape[dim] - width, None, axis=dim), axis, forward
        )
        high = lax.ppermute(lax.slice_in_dim(block, 0, width, axis=dim), axis, backward)
        block = jnp.concatenate([low, block, high], axis=dim)
    return block


def project(vector, direction):
    result = jnp.zeros_like(vector[0])
    for component in range(3):
        factor = VELOCITIES[direction][component]
        if factor != 0:
            result = result + factor * vector[component]
    return result


def moments(populations):
    density = jnp.sum(populations, axis=0)
    parts_list = []
    for component in range(3):
        result = jnp.zeros_like(density)
        for direction in range(19):
            factor = VELOCITIES[direction][component]
            if factor != 0:
                result = result + factor * populations[direction]
        parts_list.append(result / density)
    return (density, jnp.stack(parts_list))


def collide(populations, density, velocity, forcing):
    shifted = velocity + forcing / (2.0 * density)
    squared = shifted[0] * shifted[0] + shifted[1] * shifted[1] + shifted[2] * shifted[2]
    power = shifted[0] * forcing[0] + shifted[1] * forcing[1] + shifted[2] * forcing[2]
    outputs = []
    for direction in range(19):
        speed_along = project(shifted, direction)
        force_along = project(forcing, direction)
        equilibrium = (
            WEIGHTS[direction]
            * density
            * (1.0 + 3.0 * speed_along + 4.5 * speed_along * speed_along - 1.5 * squared)
        )
        source = (
            (1.0 - 0.5 * OMEGA)
            * WEIGHTS[direction]
            * (3.0 * (force_along - power) + 9.0 * speed_along * force_along)
        )
        current = populations[direction]
        outputs.append(current - OMEGA * (current - equilibrium) + source)
    return jnp.stack(outputs)


def corner_weights(fractions, alive):
    factors = []
    for corner in range(8):
        product = alive
        for axis_number, bit_value in ((0, corner // 4), (1, corner // 2 % 2), (2, corner % 2)):
            if bit_value:
                product = product * fractions[:, axis_number]
            else:
                product = product * (1.0 - fractions[:, axis_number])
        factors.append(product)
    return jnp.stack(factors, axis=1)


def stream(extended, flag_rim, post):
    width_x = post.shape[1]
    width_y = post.shape[2]
    outputs = []
    for direction in range(19):
        east_step, north_step, upward_step = VELOCITIES[direction]
        first_x = 1 - east_step
        first_y = 1 - north_step
        pulled = jnp.roll(
            extended[direction, first_x : first_x + width_x, first_y : first_y + width_y],
            upward_step,
            axis=-1,
        )
        solid = jnp.roll(
            flag_rim[first_x : first_x + width_x, first_y : first_y + width_y], upward_step, axis=-1
        )
        outputs.append(jnp.where(solid == 1, post[OPPOSITE[direction]], pulled))
    return jnp.stack(outputs)


def body(
    populations,
    flags,
    block_tile,
    marker_cell,
    marker_frac,
    marker_live,
    marker_target,
    marker_force,
):
    tile_count = lax.axis_size("gx")
    width_x, width_y, depth = (populations.shape[1], populations.shape[2], populations.shape[3])
    markers = marker_cell.shape[1]
    slot_total = tile_count * SLOT
    columns = width_x * width_y
    tile_of = block_tile[:, 0]
    onehot = (tile_of[:, None] == jnp.arange(tile_count, dtype=jnp.int32)[None, :]).astype(
        jnp.int32
    )
    ranks = jnp.sum((jnp.cumsum(onehot, axis=0) - onehot) * onehot, axis=1)
    destination = tile_of * SLOT + ranks
    live_float = marker_live.astype(jnp.float32)[:, None, :]
    cells_out = jnp.zeros((slot_total, markers), jnp.int32).at[destination].set(marker_cell)
    slot_cells = lax.all_to_all(cells_out, "gx", split_axis=0, concat_axis=0, tiled=True)
    weights = corner_weights(marker_frac, live_float[:, 0])
    weights_out = jnp.zeros((slot_total, 8, markers), jnp.float32).at[destination].set(weights)
    slot_weights = lax.all_to_all(weights_out, "gx", split_axis=0, concat_axis=0, tiled=True)
    flat_cells = slot_cells.reshape(-1)
    flat_weights = slot_weights.transpose(1, 0, 2).reshape(8, -1)
    cell_x = flat_cells // (width_y * depth)
    cell_y = flat_cells // depth % width_y
    cell_z = flat_cells % depth
    column_ids = jnp.arange(columns, dtype=jnp.int32)[:, None]
    depth_ids = jnp.arange(depth, dtype=jnp.int32)[:, None]
    column_tables = []
    depth_tables = []
    for upper in range(2):
        table = jnp.zeros((columns, flat_cells.shape[0]), jnp.float32)
        for east_bit in range(2):
            for north_bit in range(2):
                target_column = (cell_x + east_bit) * width_y + cell_y + north_bit
                table = jnp.where(
                    column_ids == target_column[None, :],
                    flat_weights[4 * east_bit + 2 * north_bit + upper][None, :],
                    table,
                )
        column_tables.append(table)
        depth_tables.append((depth_ids == (cell_z + upper)[None, :]).astype(jnp.float32))
    flag_rim = with_halo(flags, (("gx", 0), ("gy", 1)), 1)
    owner_force = marker_force
    state = populations
    for step_number in range(STEPS):
        density, velocity = moments(state)
        velocity_rows = velocity.reshape(3 * columns, depth)
        sampled_flat = jnp.zeros((3, flat_cells.shape[0]), jnp.float32)
        for upper in range(2):
            picked = jnp.dot(
                velocity_rows,
                depth_tables[upper],
                precision=HIGHEST,
                preferred_element_type=jnp.float32,
            )
            sampled_flat = sampled_flat + jnp.sum(
                picked.reshape(3, columns, -1) * column_tables[upper][None], axis=1
            )
        sampled = sampled_flat.reshape(3, slot_total, markers).transpose(1, 0, 2)
        returned = lax.all_to_all(sampled, "gx", split_axis=0, concat_axis=0, tiled=True)
        owner_force = owner_force + live_float * (marker_target - returned[destination])
        pushed = jnp.zeros((slot_total, 3, markers), jnp.float32).at[destination].set(owner_force)
        slot_force = lax.all_to_all(pushed, "gx", split_axis=0, concat_axis=0, tiled=True)
        force_flat = slot_force.transpose(1, 0, 2).reshape(3, -1)
        field = jnp.zeros((3 * columns, depth), jnp.float32)
        for upper in range(2):
            spread = (column_tables[upper][None] * force_flat[:, None, :]).reshape(3 * columns, -1)
            field = field + lax.dot_general(
                spread,
                depth_tables[upper],
                (((1,), (1,)), ((), ())),
                precision=HIGHEST,
                preferred_element_type=jnp.float32,
            )
        field = field.reshape(3, width_x, width_y, depth)
        post = collide(state, density, velocity, field)
        extended = with_halo(post, (("gx", 1), ("gy", 2)), 1)
        state = stream(extended, flag_rim, post)
    return (state, owner_force)


def solution(mesh):
    in_specs = (
        P(None, "gx", "gy", None),
        P("gx", "gy", None),
        P(("gx", "gy"), None),
        P(("gx", "gy"), None),
        P(("gx", "gy"), None, None),
        P(("gx", "gy"), None),
        P(("gx", "gy"), None, None),
        P(("gx", "gy"), None, None),
    )
    out_specs = (P(None, "gx", "gy", None), P(("gx", "gy"), None, None))
    return jax.shard_map(body, mesh=mesh, in_specs=in_specs, out_specs=out_specs, check_vma=False)
```

profile of v0, /device:TPU:7, one launch (start us, length us, event | category | flops | bytes accessed | tf_op | source)
XLA Modules:
  0.0 166.9 jit_solution(2370793500641037052)
XLA Ops:
  4.3 10.9 %all-to-all-start = ((s32[16,2,128]{2,1,0:T(2,128)}), s32[16,2,128]{2,1,0:T(2,128)S(1)}, u32[]{:S(2)}, u32[]{:S(2)}) async-start(s32[16,2,128]{2,1,0:T(2,128)} %bitcast.4), calls=%async_computation | async-start | bytes 32768 | tf_op jit(solution)/shard_map/all_to_all | solution.py:152
  15.9 2.9 %collective-permute-start = (s32[1,8,128]{2,1,0:T(8,128)S(1)}, s32[1,8,128]{2,1,0:T(8,128)S(1)}, u32[]{:S(2)}, u32[]{:S(2)}) collective-permute-start(s32[1,8,128]{2,1,0:T(8,128)S(1)} %get-tuple-element.252), channel_id=1, source_target_pairs={{0,16},{16,32},{32,48},{48,64},{64,80},{80,96},{96,112},{112,128},... | collective-permute-start | bytes 12296 | tf_op jit(solution)/shard_map/ppermute | solution.py:43
  18.8 2.2 %collective-permute-start.2 = (s32[1,8,128]{2,1,0:T(8,128)S(1)}, s32[1,8,128]{2,1,0:T(8,128)S(1)}, u32[]{:S(2)}, u32[]{:S(2)}) collective-permute-start(s32[1,8,128]{2,1,0:T(8,128)S(1)} %get-tuple-element.251), channel_id=1, source_target_pairs={{16,0},{32,16},{48,32},{64,48},{80,64},{96,80},{112,96},{128,112},... | collective-permute-start | bytes 12296 | tf_op jit(solution)/shard_map/ppermute | solution.py:46
  33.0 2.1 %scatter_fusion = f32[32,8,128]{2,1,0:T(8,128)} fusion(f32[32,8,128]{2,1,0:T(8,128)} %broadcast_in_dim.96, s32[16]{0:T(128)S(1)} %fusion.581, f32[16,8,128]{2,1,0:T(8,128)S(1)} %copy.40), kind=kCustom, calls=%fused_computation.3 | custom fusion | bytes 196672 | tf_op jit(solution)/shard_map/scatter | solution.py:154
  35.4 7.0 %all-to-all-start.1 = ((f32[32,8,128]{2,1,0:T(8,128)}), f32[32,8,128]{2,1,0:T(8,128)S(1)}, u32[]{:S(2)}, u32[]{:S(2)}) async-start(f32[32,8,128]{2,1,0:T(8,128)} %scatter_fusion), calls=%async_computation.1 | async-start | bytes 262144 | tf_op jit(solution)/shard_map/all_to_all | solution.py:155
  42.5 9.9 %all-to-all-done.1 = f32[32,8,128]{2,1,0:T(8,128)S(1)} async-done(((f32[32,8,128]{2,1,0:T(8,128)}), f32[32,8,128]{2,1,0:T(8,128)S(1)}, u32[]{:S(2)}, u32[]{:S(2)}) %all-to-all-start.1) | async-done | bytes 131104 | tf_op jit(solution)/shard_map/all_to_all | solution.py:155
  55.5 3.5 %all-to-all-start.2 = ((f32[32,3,128]{2,1,0:T(4,128)}), f32[32,3,128]{2,1,0:T(4,128)S(1)}, u32[]{:S(2)}, u32[]{:S(2)}) async-start(f32[32,3,128]{2,1,0:T(4,128)} %add_bitcast_fusion.1), calls=%async_computation.2 | async-start | bytes 131072 | tf_op jit(solution)/shard_map/all_to_all | solution.py:195
  59.1 3.5 %collective-permute-start.4 = (s32[6,1,128]{2,1,0:T(1,128)S(1)}, s32[6,1,128]{2,1,0:T(1,128)S(1)}, u32[]{:S(2)}, u32[]{:S(2)}) collective-permute-start(s32[6,1,128]{2,1,0:T(1,128)S(1)} %get-tuple-element.183), channel_id=1, source_target_pairs={{0,1},{1,2},{2,3},{3,4},{4,5},{5,6},{6,7},{7,8},{8,9},{9,10},{10,1... | collective-permute-start | bytes 9224 | tf_op jit(solution)/shard_map/ppermute | solution.py:43
  62.6 5.9 %all-to-all-done.2 = f32[32,3,128]{2,1,0:T(4,128)S(1)} async-done(((f32[32,3,128]{2,1,0:T(4,128)}), f32[32,3,128]{2,1,0:T(4,128)S(1)}, u32[]{:S(2)}, u32[]{:S(2)}) %all-to-all-start.2) | async-done | bytes 49184 | tf_op jit(solution)/shard_map/all_to_all | solution.py:195
  69.8 2.2 %scatter_fusion.1 = f32[32,3,128]{2,1,0:T(4,128)} fusion(f32[32,3,128]{2,1,0:T(4,128)} %broadcast.4701.clone, s32[16]{0:T(128)S(1)} %fusion.581, f32[16,3,128]{2,1,0:T(4,128)S(1)} %fusion.35), kind=kCustom, calls=%fused_computation.4 | custom fusion | bytes 73792 | tf_op jit(solution)/shard_map/scatter | solution.py:197
  71.9 4.0 %all-to-all-start.3 = ((f32[32,3,128]{2,1,0:T(4,128)}), f32[32,3,128]{2,1,0:T(4,128)S(1)}, u32[]{:S(2)}, u32[]{:S(2)}) async-start(f32[32,3,128]{2,1,0:T(4,128)} %scatter_fusion.1), calls=%async_computation.3 | async-start | bytes 131072 | tf_op jit(solution)/shard_map/all_to_all | solution.py:198
  76.0 9.3 %all-to-all-done.3 = f32[32,3,128]{2,1,0:T(4,128)S(1)} async-done(((f32[32,3,128]{2,1,0:T(4,128)}), f32[32,3,128]{2,1,0:T(4,128)S(1)}, u32[]{:S(2)}, u32[]{:S(2)}) %all-to-all-start.3) | async-done | bytes 49184 | tf_op jit(solution)/shard_map/all_to_all | solution.py:198
  89.6 4.7 %collective-permute-start.3 = (f32[19,1,8,128]{3,2,1,0:T(8,128)S(1)}, f32[19,1,8,128]{3,2,1,0:T(8,128)S(1)}, u32[]{:S(2)}, u32[]{:S(2)}) collective-permute-start(f32[19,1,8,128]{3,2,1,0:T(8,128)S(1)} %get-tuple-element.154), channel_id=1, source_target_pairs={{16,0},{32,16},{48,32},{64,48},{80,64},{96,80},{112,96},{128,112},... | collective-permute-start | bytes 233480 | tf_op jit(solution)/shard_map/ppermute | solution.py:46
  94.4 1.7 %collective-permute-done.1 = f32[19,1,8,128]{3,2,1,0:T(8,128)S(1)} collective-permute-done((f32[19,1,8,128]{3,2,1,0:T(8,128)S(1)}, f32[19,1,8,128]{3,2,1,0:T(8,128)S(1)}, u32[]{:S(2)}, u32[]{:S(2)}) %collective-permute-start.1) | collective-permute-done | bytes 77856 | tf_op jit(solution)/shard_map/ppermute | solution.py:43
  96.4 6.5 %collective-permute-start.5 = (f32[19,6,1,128]{3,2,1,0:T(1,128)S(1)}, f32[19,6,1,128]{3,2,1,0:T(1,128)S(1)}, u32[]{:S(2)}, u32[]{:S(2)}) collective-permute-start(f32[19,6,1,128]{3,2,1,0:T(1,128)S(1)} %get-tuple-element.140), channel_id=1, source_target_pairs={{0,1},{1,2},{2,3},{3,4},{4,5},{5,6},{6,7},{7,8},{8,9},{9,10},{10,1... | collective-permute-start | bytes 175112 | tf_op jit(solution)/shard_map/ppermute | solution.py:43
  104.1 4.5 %collective-permute-done.7 = f32[19,6,1,128]{3,2,1,0:T(1,128)S(1)} collective-permute-done((f32[19,6,1,128]{3,2,1,0:T(1,128)S(1)}, f32[19,6,1,128]{3,2,1,0:T(1,128)S(1)}, u32[]{:S(2)}, u32[]{:S(2)}) %collective-permute-start.7) | collective-permute-done | bytes 58400 | tf_op jit(solution)/shard_map/ppermute | solution.py:46
  112.0 16.5 %all_to_all.34 = f32[32,3,128]{2,1,0:T(4,128)S(1)} all-to-all(f32[32,3,128]{2,1,0:T(4,128)S(1)} %add_bitcast_fusion), channel_id=1, replica_groups=mesh['gx'=16,'gy'=16] {'gx'}, dimensions={0} | all-to-all | bytes 98304 | tf_op jit(solution)/shard_map/all_to_all | solution.py:195
  129.8 2.2 %scatter_fusion.2 = f32[32,3,128]{2,1,0:T(4,128)} fusion(f32[32,3,128]{2,1,0:T(4,128)} %broadcast.4701, s32[16]{0:T(128)S(1)} %fusion.581, f32[16,3,128]{2,1,0:T(4,128)S(1)} %fusion.37), kind=kCustom, calls=%fused_computation.5 | custom fusion | bytes 73792 | tf_op jit(solution)/shard_map/scatter | solution.py:197
  131.9 3.5 %all-to-all-start.5 = ((f32[32,3,128]{2,1,0:T(4,128)}), f32[32,3,128]{2,1,0:T(4,128)S(1)}, u32[]{:S(2)}, u32[]{:S(2)}) async-start(f32[32,3,128]{2,1,0:T(4,128)} %scatter_fusion.2), calls=%async_computation.5 | async-start | bytes 131072 | tf_op jit(solution)/shard_map/all_to_all | solution.py:198
  136.1 8.8 %all-to-all-done.5 = f32[32,3,128]{2,1,0:T(4,128)S(1)} async-done(((f32[32,3,128]{2,1,0:T(4,128)}), f32[32,3,128]{2,1,0:T(4,128)S(1)}, u32[]{:S(2)}, u32[]{:S(2)}) %all-to-all-start.5) | async-done | bytes 49184 | tf_op jit(solution)/shard_map/all_to_all | solution.py:198
  149.1 4.8 %collective-permute-start.9 = (f32[19,1,8,128]{3,2,1,0:T(8,128)S(1)}, f32[19,1,8,128]{3,2,1,0:T(8,128)S(1)}, u32[]{:S(2)}, u32[]{:S(2)}) collective-permute-start(f32[19,1,8,128]{3,2,1,0:T(8,128)S(1)} %get-tuple-element.151), channel_id=1, source_target_pairs={{16,0},{32,16},{48,32},{64,48},{80,64},{96,80},{112,96},{128,112},... | collective-permute-start | bytes 233480 | tf_op jit(solution)/shard_map/ppermute | solution.py:46
  154.0 2.6 %collective-permute-done.8 = f32[19,1,8,128]{3,2,1,0:T(8,128)S(1)} collective-permute-done((f32[19,1,8,128]{3,2,1,0:T(8,128)S(1)}, f32[19,1,8,128]{3,2,1,0:T(8,128)S(1)}, u32[]{:S(2)}, u32[]{:S(2)}) %collective-permute-start.8) | collective-permute-done | bytes 77856 | tf_op jit(solution)/shard_map/ppermute | solution.py:43
  156.7 2.3 %collective-permute-start.10 = (f32[19,6,1,128]{3,2,1,0:T(1,128)S(1)}, f32[19,6,1,128]{3,2,1,0:T(1,128)S(1)}, u32[]{:S(2)}, u32[]{:S(2)}) collective-permute-start(f32[19,6,1,128]{3,2,1,0:T(1,128)S(1)} %get-tuple-element.136), channel_id=1, source_target_pairs={{0,1},{1,2},{2,3},{3,4},{4,5},{5,6},{6,7},{7,8},{8,9},{9,10},{10,1... | collective-permute-start | bytes 175112 | tf_op jit(solution)/shard_map/ppermute | solution.py:43
  160.2 4.4 %collective-permute-done.11 = f32[19,6,1,128]{3,2,1,0:T(1,128)S(1)} collective-permute-done((f32[19,6,1,128]{3,2,1,0:T(1,128)S(1)}, f32[19,6,1,128]{3,2,1,0:T(1,128)S(1)}, u32[]{:S(2)}, u32[]{:S(2)}) %collective-permute-start.11) | collective-permute-done | bytes 58400 | tf_op jit(solution)/shard_map/ppermute | solution.py:46
  (191 shorter events, 39.8 us)
Async XLA Ops:
  0.6 34.6 %copy-start.1 = (s32[4,8,128]{2,1,0:T(8,128)S(1)}, s32[4,8,128]{2,1,0:T(8,128)}, u32[]{:S(2)}) copy-start(s32[4,8,128]{2,1,0:T(8,128)} %param.9) | copy-start | bytes 49156
  0.6 31.7 %copy-start.3 = (s32[16,128]{1,0:T(8,128)S(1)}, s32[16,128]{1,0:T(8,128)}, u32[]{:S(2)}) copy-start(s32[16,128]{1,0:T(8,128)} %param.13) | copy-start | bytes 24580
  4.3 31.2 %all-to-all-start = ((s32[16,2,128]{2,1,0:T(2,128)}), s32[16,2,128]{2,1,0:T(2,128)S(1)}, u32[]{:S(2)}, u32[]{:S(2)}) async-start(s32[16,2,128]{2,1,0:T(2,128)} %bitcast.4), calls=%async_computation | async-start | bytes 32768 | tf_op jit(solution)/shard_map/all_to_all | solution.py:152
  15.9 19.3 %collective-permute-start = (s32[1,8,128]{2,1,0:T(8,128)S(1)}, s32[1,8,128]{2,1,0:T(8,128)S(1)}, u32[]{:S(2)}, u32[]{:S(2)}) collective-permute-start(s32[1,8,128]{2,1,0:T(8,128)S(1)} %get-tuple-element.252), channel_id=1, source_target_pairs={{0,16},{16,32},{32,48},{48,64},{64,80},{80,96},{96,112},{112,128},... | collective-permute-start | bytes 12296 | tf_op jit(solution)/shard_map/ppermute | solution.py:43
  18.8 16.6 %collective-permute-start.2 = (s32[1,8,128]{2,1,0:T(8,128)S(1)}, s32[1,8,128]{2,1,0:T(8,128)S(1)}, u32[]{:S(2)}, u32[]{:S(2)}) collective-permute-start(s32[1,8,128]{2,1,0:T(8,128)S(1)} %get-tuple-element.251), channel_id=1, source_target_pairs={{16,0},{32,16},{48,32},{64,48},{80,64},{96,80},{112,96},{128,112},... | collective-permute-start | bytes 12296 | tf_op jit(solution)/shard_map/ppermute | solution.py:46
  35.4 16.9 %all-to-all-start.1 = ((f32[32,8,128]{2,1,0:T(8,128)}), f32[32,8,128]{2,1,0:T(8,128)S(1)}, u32[]{:S(2)}, u32[]{:S(2)}) async-start(f32[32,8,128]{2,1,0:T(8,128)} %scatter_fusion), calls=%async_computation.1 | async-start | bytes 262144 | tf_op jit(solution)/shard_map/all_to_all | solution.py:155
  52.7 16.3 %copy-start.4 = (f32[16,3,128]{2,0,1:T(8,128)S(1)}, f32[16,3,128]{2,0,1:T(8,128)}, u32[]{:S(2)}) copy-start(f32[16,3,128]{2,0,1:T(8,128)} %param.14) | copy-start | bytes 73732
  52.7 16.3 %copy-start.5 = (f32[16,3,128]{2,0,1:T(8,128)S(1)}, f32[16,3,128]{2,0,1:T(8,128)}, u32[]{:S(2)}) copy-start(f32[16,3,128]{2,0,1:T(8,128)} %param.15) | copy-start | bytes 73732
  55.5 12.9 %all-to-all-start.2 = ((f32[32,3,128]{2,1,0:T(4,128)}), f32[32,3,128]{2,1,0:T(4,128)S(1)}, u32[]{:S(2)}, u32[]{:S(2)}) async-start(f32[32,3,128]{2,1,0:T(4,128)} %add_bitcast_fusion.1), calls=%async_computation.2 | async-start | bytes 131072 | tf_op jit(solution)/shard_map/all_to_all | solution.py:195
  59.1 16.8 %collective-permute-start.4 = (s32[6,1,128]{2,1,0:T(1,128)S(1)}, s32[6,1,128]{2,1,0:T(1,128)S(1)}, u32[]{:S(2)}, u32[]{:S(2)}) collective-permute-start(s32[6,1,128]{2,1,0:T(1,128)S(1)} %get-tuple-element.183), channel_id=1, source_target_pairs={{0,1},{1,2},{2,3},{3,4},{4,5},{5,6},{6,7},{7,8},{8,9},{9,10},{10,1... | collective-permute-start | bytes 9224 | tf_op jit(solution)/shard_map/ppermute | solution.py:43
  62.6 13.3 %collective-permute-start.6 = (s32[6,1,128]{2,1,0:T(1,128)S(1)}, s32[6,1,128]{2,1,0:T(1,128)S(1)}, u32[]{:S(2)}, u32[]{:S(2)}) collective-permute-start(s32[6,1,128]{2,1,0:T(1,128)S(1)} %get-tuple-element.182), channel_id=1, source_target_pairs={{1,0},{2,1},{3,2},{4,3},{5,4},{6,5},{7,6},{8,7},{9,8},{10,9},{11,1... | collective-permute-start | bytes 9224 | tf_op jit(solution)/shard_map/ppermute | solution.py:46
  71.9 13.4 %all-to-all-start.3 = ((f32[32,3,128]{2,1,0:T(4,128)}), f32[32,3,128]{2,1,0:T(4,128)S(1)}, u32[]{:S(2)}, u32[]{:S(2)}) async-start(f32[32,3,128]{2,1,0:T(4,128)} %scatter_fusion.1), calls=%async_computation.3 | async-start | bytes 131072 | tf_op jit(solution)/shard_map/all_to_all | solution.py:198
  85.6 2.8 %copy-start = (f32[19,4,8,128]{3,2,1,0:T(8,128)S(1)}, f32[19,4,8,128]{3,2,1,0:T(8,128)}, u32[]{:S(2)}) copy-start(f32[19,4,8,128]{3,2,1,0:T(8,128)} %param.8) | copy-start | bytes 933892
  89.0 7.1 %collective-permute-start.1 = (f32[19,1,8,128]{3,2,1,0:T(8,128)S(1)}, f32[19,1,8,128]{3,2,1,0:T(8,128)S(1)}, u32[]{:S(2)}, u32[]{:S(2)}) collective-permute-start(f32[19,1,8,128]{3,2,1,0:T(8,128)S(1)} %get-tuple-element.155), channel_id=1, source_target_pairs={{0,16},{16,32},{32,48},{48,64},{64,80},{80,96},{96,112},{112,128},... | collective-permute-start | bytes 233480 | tf_op jit(solution)/shard_map/ppermute | solution.py:43
  89.6 6.5 %collective-permute-start.3 = (f32[19,1,8,128]{3,2,1,0:T(8,128)S(1)}, f32[19,1,8,128]{3,2,1,0:T(8,128)S(1)}, u32[]{:S(2)}, u32[]{:S(2)}) collective-permute-start(f32[19,1,8,128]{3,2,1,0:T(8,128)S(1)} %get-tuple-element.154), channel_id=1, source_target_pairs={{16,0},{32,16},{48,32},{64,48},{80,64},{96,80},{112,96},{128,112},... | collective-permute-start | bytes 233480 | tf_op jit(solution)/shard_map/ppermute | solution.py:46
  96.4 7.8 %collective-permute-start.5 = (f32[19,6,1,128]{3,2,1,0:T(1,128)S(1)}, f32[19,6,1,128]{3,2,1,0:T(1,128)S(1)}, u32[]{:S(2)}, u32[]{:S(2)}) collective-permute-start(f32[19,6,1,128]{3,2,1,0:T(1,128)S(1)} %get-tuple-element.140), channel_id=1, source_target_pairs={{0,1},{1,2},{2,3},{3,4},{4,5},{5,6},{6,7},{7,8},{8,9},{9,10},{10,1... | collective-permute-start | bytes 175112 | tf_op jit(solution)/shard_map/ppermute | solution.py:43
  102.9 5.7 %collective-permute-start.7 = (f32[19,6,1,128]{3,2,1,0:T(1,128)S(1)}, f32[19,6,1,128]{3,2,1,0:T(1,128)S(1)}, u32[]{:S(2)}, u32[]{:S(2)}) collective-permute-start(f32[19,6,1,128]{3,2,1,0:T(1,128)S(1)} %get-tuple-element.139), channel_id=1, source_target_pairs={{1,0},{2,1},{3,2},{4,3},{5,4},{6,5},{7,6},{8,7},{9,8},{10,9},{11,1... | collective-permute-start | bytes 175112 | tf_op jit(solution)/shard_map/ppermute | solution.py:46
  131.9 12.9 %all-to-all-start.5 = ((f32[32,3,128]{2,1,0:T(4,128)}), f32[32,3,128]{2,1,0:T(4,128)S(1)}, u32[]{:S(2)}, u32[]{:S(2)}) async-start(f32[32,3,128]{2,1,0:T(4,128)} %scatter_fusion.2), calls=%async_computation.5 | async-start | bytes 131072 | tf_op jit(solution)/shard_map/all_to_all | solution.py:198
  148.7 7.9 %collective-permute-start.8 = (f32[19,1,8,128]{3,2,1,0:T(8,128)S(1)}, f32[19,1,8,128]{3,2,1,0:T(8,128)S(1)}, u32[]{:S(2)}, u32[]{:S(2)}) collective-permute-start(f32[19,1,8,128]{3,2,1,0:T(8,128)S(1)} %get-tuple-element.152), channel_id=1, source_target_pairs={{0,16},{16,32},{32,48},{48,64},{64,80},{80,96},{96,112},{112,128},... | collective-permute-start | bytes 233480 | tf_op jit(solution)/shard_map/ppermute | solution.py:43
  149.1 7.5 %collective-permute-start.9 = (f32[19,1,8,128]{3,2,1,0:T(8,128)S(1)}, f32[19,1,8,128]{3,2,1,0:T(8,128)S(1)}, u32[]{:S(2)}, u32[]{:S(2)}) collective-permute-start(f32[19,1,8,128]{3,2,1,0:T(8,128)S(1)} %get-tuple-element.151), channel_id=1, source_target_pairs={{16,0},{32,16},{48,32},{64,48},{80,64},{96,80},{112,96},{128,112},... | collective-permute-start | bytes 233480 | tf_op jit(solution)/shard_map/ppermute | solution.py:46
  156.7 3.5 %collective-permute-start.10 = (f32[19,6,1,128]{3,2,1,0:T(1,128)S(1)}, f32[19,6,1,128]{3,2,1,0:T(1,128)S(1)}, u32[]{:S(2)}, u32[]{:S(2)}) collective-permute-start(f32[19,6,1,128]{3,2,1,0:T(1,128)S(1)} %get-tuple-element.136), channel_id=1, source_target_pairs={{0,1},{1,2},{2,3},{3,4},{4,5},{5,6},{6,7},{7,8},{8,9},{9,10},{10,1... | collective-permute-start | bytes 175112 | tf_op jit(solution)/shard_map/ppermute | solution.py:43
  159.0 5.7 %collective-permute-start.11 = (f32[19,6,1,128]{3,2,1,0:T(1,128)S(1)}, f32[19,6,1,128]{3,2,1,0:T(1,128)S(1)}, u32[]{:S(2)}, u32[]{:S(2)}) collective-permute-start(f32[19,6,1,128]{3,2,1,0:T(1,128)S(1)} %get-tuple-element.135), channel_id=1, source_target_pairs={{1,0},{2,1},{3,2},{4,3},{5,4},{6,5},{7,6},{8,7},{9,8},{10,9},{11,1... | collective-permute-start | bytes 175112 | tf_op jit(solution)/shard_map/ppermute | solution.py:46
  166.2 0.7 copy-start.2
where the time goes:
time: 169 us; the launch traced here: 167 us
  starting transfers between devices  56.7 us (34%)
  waiting for transfers between devices  49.5 us (29%)
  local copies, waits for them, and re-layouts  16.7 us (10%)
  blocking collectives  16.5 us (10%)
  other arithmetic  16.3 us (10%)
  matrix products  9.85 us (6%)
    all_to_all x2, waiting for transfers between devices, body(): lax.all_to_all(pushed, 'gx', split_axis=0, concat_axis=0, tiled=True)  18.1 us
    all_to_all x1, blocking collectives, body(): lax.all_to_all(sampled, 'gx', split_axis=0, concat_axis=0, tiled=True)  16.5 us
    ppermute x6, starting transfers between devices, with_halo(): lax.ppermute(lax.slice_in_dim(block, block.shape[dim] - width, None, axis...  16.1 us
    ppermute x6, starting transfers between devices, with_halo(): lax.ppermute(lax.slice_in_dim(block, 0, width, axis=dim), axis, backward)  11.7 us
    all_to_all x1, starting transfers between devices, body(): lax.all_to_all(cells_out, 'gx', split_axis=0, concat_axis=0, tiled=True)  10.9 us
    all_to_all x1, waiting for transfers between devices, body(): lax.all_to_all(weights_out, 'gx', split_axis=0, concat_axis=0, tiled=True)  9.87 us
    ppermute x6, waiting for transfers between devices, with_halo(): lax.ppermute(lax.slice_in_dim(block, 0, width, axis=dim), axis, backward)  8.92 us
    all_to_all x2, starting transfers between devices, body(): lax.all_to_all(pushed, 'gx', split_axis=0, concat_axis=0, tiled=True)  7.48 us
  transfers between devices with their start and end apart: 17, of which 10 were waited for; matrix products, arithmetic and copies ran while one was open for 12% of the time, Pallas kernels for 0%

commit v1 on v0

v1 whole, which is shorter than its diff:
```python
import functools

import jax
import jax.numpy as jnp
from jax import lax
from jax.experimental import pallas as pl
from jax.experimental.pallas import tpu as pltpu
from jax.sharding import PartitionSpec as P

STEPS = 2
SLOT = 2
MESH = pl.DeviceIdType.MESH

VELOCITIES = (
    (0, 0, 0),
    (1, 0, 0),
    (-1, 0, 0),
    (0, 1, 0),
    (0, -1, 0),
    (0, 0, 1),
    (0, 0, -1),
    (1, 1, 0),
    (-1, -1, 0),
    (1, -1, 0),
    (-1, 1, 0),
    (1, 0, 1),
    (-1, 0, -1),
    (1, 0, -1),
    (-1, 0, 1),
    (0, 1, 1),
    (0, -1, -1),
    (0, 1, -1),
    (0, -1, 1),
)
OPPOSITE = (0, 2, 1, 4, 3, 6, 5, 8, 7, 10, 9, 12, 11, 14, 13, 16, 15, 18, 17)
WEIGHTS = (1.0 / 3.0,) + (1.0 / 18.0,) * 6 + (1.0 / 36.0,) * 12
OMEGA = 1.25

EAST = tuple(d for d in range(19) if VELOCITIES[d][0] == 1)
WEST = tuple(d for d in range(19) if VELOCITIES[d][0] == -1)
NORTH = tuple(d for d in range(19) if VELOCITIES[d][1] == 1)
SOUTH = tuple(d for d in range(19) if VELOCITIES[d][1] == -1)
XDIRS = {1: EAST, -1: WEST}
YDIRS = {1: NORTH, -1: SOUTH}
CORNERS = ((1, 1), (-1, -1), (1, -1), (-1, 1))
CORNER_DIR = {(1, 1): 7, (-1, -1): 8, (1, -1): 9, (-1, 1): 10}

CX, CY, NZ = 4, 8, 128
COLS = CX * CY


def dot_product(direction, vector):
    total = None
    for component in range(3):
        factor = VELOCITIES[direction][component]
        if factor != 0:
            term = vector[component] if factor == 1 else -vector[component]
            total = term if total is None else total + term
    return total


def moments(f):
    density = f[0]
    for d in range(1, 19):
        density = density + f[d]
    parts = []
    for component in range(3):
        plus = minus = None
        for d in range(19):
            factor = VELOCITIES[d][component]
            if factor == 1:
                plus = f[d] if plus is None else plus + f[d]
            elif factor == -1:
                minus = f[d] if minus is None else minus + f[d]
        parts.append(plus - minus)
    inverse = 1.0 / density
    return density, inverse, [part * inverse for part in parts]


def collide(f, density, inverse, velocity, field):
    half = 0.5 * inverse
    shifted = [velocity[c] + field[c] * half for c in range(3)]
    squared = shifted[0] * shifted[0] + shifted[1] * shifted[1] + shifted[2] * shifted[2]
    power = shifted[0] * field[0] + shifted[1] * field[1] + shifted[2] * field[2]
    gain = 1.0 - 0.5 * OMEGA
    scaled = OMEGA * density
    base = scaled * (1.0 - 1.5 * squared) - (3.0 * gain) * power
    curved = 4.5 * scaled
    sloped = 3.0 * scaled
    post = [None] * 19
    post[0] = (1.0 - OMEGA) * f[0] + WEIGHTS[0] * base
    for d in range(1, 19, 2):
        s = dot_product(d, shifted)
        g = dot_product(d, field)
        even = base + s * (curved * s + (9.0 * gain) * g)
        odd = sloped * s + (3.0 * gain) * g
        post[d] = (1.0 - OMEGA) * f[d] + WEIGHTS[d] * (even + odd)
        post[d + 1] = (1.0 - OMEGA) * f[d + 1] + WEIGHTS[d] * (even - odd)
    return post


def kernel(
    n_gx,
    n_gy,
    pop_hbm,
    flags_hbm,
    tile_hbm,
    cell_hbm,
    frac_hbm,
    live_hbm,
    target_hbm,
    force_hbm,
    pop_out,
    force_out,
    state,
    post,
    flags_v,
    tile_s,
    cell_v,
    frac_v,
    live_v,
    target_v,
    force_v,
    send_a,
    recv_a,
    send_b,
    recv_b,
    send_r,
    recv_r,
    force_now,
    z_table,
    c_table,
    s_table,
    v_table,
    field_v,
    face_send,
    face_recv,
    edge_send,
    edge_recv,
    corner_send,
    corner_recv,
    force_res,
    in_sem,
    out_sem,
    a_send_sem,
    a_recv_sem,
    b_send_sem,
    b_recv_sem,
    r_send_sem,
    r_recv_sem,
    h_send_sem,
    h_recv_sem,
):
    gx = lax.axis_index("gx")
    gy = lax.axis_index("gy")
    blocks = cell_v.shape[0]

    def around(position, shift, count):
        return lax.rem(position + shift + count, count)

    in_pairs = (
        (tile_hbm, tile_s),
        (cell_hbm, cell_v),
        (frac_hbm, frac_v),
        (live_hbm, live_v),
        (target_hbm, target_v),
        (force_hbm, force_v),
        (pop_hbm, state),
        (flags_hbm, flags_v),
    )
    loads = [
        pltpu.make_async_copy(src, dst, in_sem.at[i]) for i, (src, dst) in enumerate(in_pairs)
    ]
    for load in loads:
        load.start()

    barrier = pltpu.get_barrier_semaphore()

    def greet(step, carry):
        pl.semaphore_signal(
            barrier,
            inc=1,
            device_id={"gx": around(gx, step, n_gx)},
            device_id_type=MESH,
        )
        return carry

    lax.fori_loop(1, n_gx, greet, 0)
    for dx in (-1, 0, 1):
        for dy in (-1, 1):
            pl.semaphore_signal(
                barrier,
                inc=1,
                device_id={"gx": around(gx, dx, n_gx), "gy": around(gy, dy, n_gy)},
                device_id_type=MESH,
            )

    for load in loads[:6]:
        load.wait()

    def pack(t, carry):
        first = jnp.int32(-1)
        second = jnp.int32(-1)
        for b in range(blocks - 1, -1, -1):
            match = tile_s[b, 0] == t
            second = jnp.where(match, first, second)
            first = jnp.where(match, jnp.int32(b), first)
        for s, index in enumerate((first, second)):
            valid = jnp.where(index >= 0, 1.0, 0.0)
            at = jnp.maximum(index, 0)
            send_a[t, 4 * s : 4 * s + 1, :] = cell_v[pl.ds(at, 1), :].astype(jnp.float32)
            send_a[t, 4 * s + 1 : 4 * s + 4, :] = frac_v[at]
            send_b[t, s, 0:3, :] = target_v[at]
            send_b[t, s, 3:6, :] = force_v[at]
            send_b[t, s, 6:7, :] = live_v[pl.ds(at, 1), :].astype(jnp.float32) * valid
            send_b[t, s, 7:8, :] = jnp.zeros((1, NZ), jnp.float32)
        return carry

    lax.fori_loop(0, n_gx, pack, 0)
    recv_a[gx] = send_a[gx]
    recv_b[gx] = send_b[gx]

    pl.semaphore_wait(barrier, n_gx - 1 + 6)

    def copy_a(to, slot):
        return pltpu.make_async_remote_copy(
            src_ref=send_a.at[to],
            dst_ref=recv_a.at[slot],
            send_sem=a_send_sem.at[to],
            recv_sem=a_recv_sem.at[slot],
            device_id={"gx": to},
            device_id_type=MESH,
        )

    def copy_b(to, slot):
        return pltpu.make_async_remote_copy(
            src_ref=send_b.at[to],
            dst_ref=recv_b.at[slot],
            send_sem=b_send_sem.at[to],
            recv_sem=b_recv_sem.at[slot],
            device_id={"gx": to},
            device_id_type=MESH,
        )

    def copy_r(to, slot):
        return pltpu.make_async_remote_copy(
            src_ref=send_r.at[to],
            dst_ref=recv_r.at[slot],
            send_sem=r_send_sem.at[to],
            recv_sem=r_recv_sem.at[slot],
            device_id={"gx": to},
            device_id_type=MESH,
        )

    def each_peer(action):
        def one(step, carry):
            action(around(gx, step, n_gx))
            return carry

        lax.fori_loop(1, n_gx, one, 0)

    each_peer(lambda peer: copy_a(peer, gx).start())
    each_peer(lambda peer: copy_b(peer, gx).start())

    for load in loads[6:]:
        load.wait()

    def velocity_tables():
        f = [state[d] for d in range(19)]
        density, inverse, velocity = moments(f)
        for c in range(3):
            rows = velocity[c].reshape(COLS, NZ)
            high = rows.astype(jnp.bfloat16)
            low = (rows - high.astype(jnp.float32)).astype(jnp.bfloat16)
            for half in range(2):
                v_table[c * COLS : (c + 1) * COLS, half * NZ : (half + 1) * NZ] = high
                v_table[(3 + c) * COLS : (4 + c) * COLS, half * NZ : (half + 1) * NZ] = low

    velocity_tables()

    each_peer(lambda peer: copy_a(gx, peer).wait_recv())

    y_rows = lax.broadcasted_iota(jnp.int32, (CY, NZ), 0)
    z_rows = lax.broadcasted_iota(jnp.int32, (16, NZ), 0)

    def build(src, carry):
        for s in range(SLOT):
            column = pl.ds(pl.multiple_of(src * (SLOT * NZ) + s * NZ, NZ), NZ)
            cell = recv_a[src, 4 * s : 4 * s + 1, :].astype(jnp.int32)
            px = recv_a[src, 4 * s + 1 : 4 * s + 2, :]
            py = recv_a[src, 4 * s + 2 : 4 * s + 3, :]
            pz = recv_a[src, 4 * s + 3 : 4 * s + 4, :]
            i = lax.shift_right_logical(cell, 10)
            j = lax.shift_right_logical(cell, 7) & 7
            k = cell & 127
            wide = (CY, NZ)
            jw = jnp.broadcast_to(j, wide)
            pyw = jnp.broadcast_to(py, wide)
            wy = jnp.where(y_rows == jw, 1.0 - pyw, jnp.where(y_rows == jw + 1, pyw, 0.0))
            for x in range(CX):
                wx = jnp.where(i == x, 1.0 - px, jnp.where(i == x - 1, px, 0.0))
                c_table[x * CY : (x + 1) * CY, column] = jnp.broadcast_to(wx, wide) * wy
            tall = (16, NZ)
            kw = jnp.broadcast_to(k, tall)
            upper = jnp.broadcast_to(pz, tall)
            lower = 1.0 - upper
            upper_high = upper.astype(jnp.bfloat16)
            lower_high = lower.astype(jnp.bfloat16)
            upper_low = (upper - upper_high.astype(jnp.float32)).astype(jnp.bfloat16)
            lower_low = (lower - lower_high.astype(jnp.float32)).astype(jnp.bfloat16)
            k16 = kw.astype(jnp.bfloat16)
            none = jnp.zeros(tall, jnp.bfloat16)
            for chunk in range(NZ // 16):
                here = (z_rows + 16 * chunk).astype(jnp.bfloat16)
                below = (z_rows + (16 * chunk - 1)).astype(jnp.bfloat16)
                is_low = here == k16
                is_up = below == k16
                z_table[16 * chunk : 16 * chunk + 16, column] = jnp.where(
                    is_low, lower_high, jnp.where(is_up, upper_high, none)
                )
                z_table[NZ + 16 * chunk : NZ + 16 * chunk + 16, column] = jnp.where(
                    is_low, lower_low, jnp.where(is_up, upper_low, none)
                )
        return carry

    lax.fori_loop(0, n_gx, build, 0)
    each_peer(lambda peer: copy_b(gx, peer).wait_recv())

    def exchange(step):
        copies = []
        number = 0
        for sx in (1, -1):
            copies.append(
                pltpu.make_async_remote_copy(
                    src_ref=face_send.at[step, 0 if sx == 1 else 1],
                    dst_ref=face_recv.at[step, 0 if sx == 1 else 1],
                    send_sem=h_send_sem.at[step, number],
                    recv_sem=h_recv_sem.at[step, number],
                    device_id={"gx": around(gx, sx, n_gx)},
                    device_id_type=MESH,
                )
            )
            number += 1
        for sy in (1, -1):
            copies.append(
                pltpu.make_async_remote_copy(
                    src_ref=edge_send.at[step, 0 if sy == 1 else 1],
                    dst_ref=edge_recv.at[step, 0 if sy == 1 else 1],
                    send_sem=h_send_sem.at[step, number],
                    recv_sem=h_recv_sem.at[step, number],
                    device_id={"gy": around(gy, sy, n_gy)},
                    device_id_type=MESH,
                )
            )
            number += 1
        for corner, (sx, sy) in enumerate(CORNERS):
            copies.append(
                pltpu.make_async_remote_copy(
                    src_ref=corner_send.at[step, corner],
                    dst_ref=corner_recv.at[step, corner],
                    send_sem=h_send_sem.at[step, number],
                    recv_sem=h_recv_sem.at[step, number],
                    device_id={"gx": around(gx, sx, n_gx), "gy": around(gy, sy, n_gy)},
                    device_id_type=MESH,
                )
            )
            number += 1
        return copies

    flags_f = flags_v[...].astype(jnp.float32)
    for side, sx in enumerate((1, -1)):
        face_send[0, side, 5] = flags_f[CX - 1 if sx == 1 else 0]
    for side, sy in enumerate((1, -1)):
        for x in range(CX):
            y = CY - 1 if sy == 1 else 0
            edge_send[0, side, 20 + x : 21 + x, :] = flags_f[x, y : y + 1, :]
    for corner, (sx, sy) in enumerate(CORNERS):
        x = CX - 1 if sx == 1 else 0
        y = CY - 1 if sy == 1 else 0
        corner_send[0, corner, 0:8, :] = jnp.zeros((8, NZ), jnp.float32)
        corner_send[1, corner, 0:8, :] = jnp.zeros((8, NZ), jnp.float32)
        corner_send[0, corner, 1:2, :] = flags_f[x, y : y + 1, :]

    sublane = lax.broadcasted_iota(jnp.int32, (CY, NZ), 0)

    def pulled(tiles, step, direction, x, dx, dy, dz):
        from_x = x - dx
        if dx != 0 and (from_x < 0 or from_x >= CX):
            side = 0 if dx == 1 else 1
            place = 5 if direction is None else XDIRS[dx].index(direction)
            tile = face_recv[step, side, place]
            outside = True
        else:
            tile = tiles[from_x]
            outside = False
        if dy != 0:
            if outside:
                corner = CORNERS.index((dx, dy))
                row = corner_recv[step, corner, (1 if direction is None else 0) :, :][0:1]
            else:
                side = 0 if dy == 1 else 1
                place = 20 if direction is None else 4 * YDIRS[dy].index(direction)
                row = edge_recv[step, side, place + from_x : place + from_x + 1, :]
            tile = pltpu.roll(tile, 1 if dy == 1 else CY - 1, 0)
            edge = 0 if dy == 1 else CY - 1
            tile = jnp.where(sublane == edge, jnp.broadcast_to(row, (CY, NZ)), tile)
        if dz != 0:
            tile = pltpu.roll(tile, 1 if dz == 1 else NZ - 1, 1)
        return tile

    for step in range(STEPS):
        last = step == STEPS - 1

        def sample(src, carry):
            wide = pl.ds(pl.multiple_of(src * (SLOT * NZ), SLOT * NZ), SLOT * NZ)
            picked = jnp.dot(
                v_table[...], z_table[:, wide], preferred_element_type=jnp.float32
            )
            weights = c_table[:, wide]
            for c in range(3):
                both = (
                    picked[c * COLS : (c + 1) * COLS]
                    + picked[(3 + c) * COLS : (4 + c) * COLS]
                ) * weights
                sampled = jnp.sum(both, axis=0, keepdims=True)
                for s in range(SLOT):
                    lanes = slice(s * NZ, (s + 1) * NZ)
                    live = recv_b[src, s, 6:7, :]
                    target = recv_b[src, s, c : c + 1, :]
                    if step == 0:
                        before = recv_b[src, s, 3 + c : 4 + c, :]
                    else:
                        before = force_now[src, 3 * s + c : 3 * s + c + 1, :]
                    after = before + live * (target - sampled[:, lanes])
                    if last:
                        send_r[src, 3 * s + c : 3 * s + c + 1, :] = after
                    else:
                        force_now[src, 3 * s + c : 3 * s + c + 1, :] = after
                    pushed = weights[:, lanes] * (live * after)
                    column = pl.ds(pl.multiple_of(src * (SLOT * NZ) + s * NZ, NZ), NZ)
                    high = pushed.astype(jnp.bfloat16)
                    low = (pushed - high.astype(jnp.float32)).astype(jnp.bfloat16)
                    s_table[c * COLS : (c + 1) * COLS, column] = high
                    s_table[(3 + c) * COLS : (4 + c) * COLS, column] = low
            if last:
                send_r[src, 6:8, :] = jnp.zeros((2, NZ), jnp.float32)
            return carry

        lax.fori_loop(0, n_gx, sample, 0)
        if last:
            recv_r[gx] = send_r[gx]
            each_peer(lambda peer: copy_r(peer, gx).start())

        spread = lax.dot_general(
            s_table[...],
            z_table[...],
            (((1,), (1,)), ((), ())),
            preferred_element_type=jnp.float32,
        )
        field = (spread[: 3 * COLS, :NZ] + spread[3 * COLS :, :NZ]) + (
            spread[: 3 * COLS, NZ:] + spread[3 * COLS :, NZ:]
        )
        field = field.reshape(3, CX, CY, NZ)
        f = [state[d] for d in range(19)]
        density, inverse, velocity = moments(f)
        after = collide(f, density, inverse, velocity, [field[c] for c in range(3)])
        for side, sx in enumerate((1, -1)):
            for place, d in enumerate(XDIRS[sx]):
                face_send[step, side, place] = after[d][CX - 1 if sx == 1 else 0]
        for side, sy in enumerate((1, -1)):
            y = CY - 1 if sy == 1 else 0
            for place, d in enumerate(YDIRS[sy]):
                for x in range(CX):
                    row = 4 * place + x
                    edge_send[step, side, row : row + 1, :] = after[d][x, y : y + 1, :]
        for corner, (sx, sy) in enumerate(CORNERS):
            x = CX - 1 if sx == 1 else 0
            y = CY - 1 if sy == 1 else 0
            corner_send[step, corner, 0:1, :] = after[CORNER_DIR[sx, sy]][x, y : y + 1, :]
        if step > 0:
            for side in range(2):
                face_send[step, side, 5] = jnp.zeros((CY, NZ), jnp.float32)
                edge_send[step, side, 20:24, :] = jnp.zeros((4, NZ), jnp.float32)
        copies = exchange(step)
        for copy in copies:
            copy.start()
        for d in range(19):
            post[d] = after[d]
        if last:
            each_peer(lambda peer: copy_r(gx, peer).wait_recv())
            for b in range(blocks):
                tile = tile_s[b, 0]
                rank = jnp.int32(0)
                for other in range(b):
                    rank = rank + jnp.where(tile_s[other, 0] == tile, 1, 0)
                whole = recv_r[tile]
                force_res[b] = jnp.where(rank == 0, whole[0:3], whole[3:6])
            force_copy = pltpu.make_async_copy(force_res, force_out, out_sem.at[0])
            force_copy.start()
        for copy in copies:
            copy.wait_recv()
        tiles_flag = [flags_v[x].astype(jnp.float32) for x in range(CX)]
        for d in range(19):
            dx, dy, dz = VELOCITIES[d]
            tiles = [post[d, x] for x in range(CX)]
            for x in range(CX):
                solid = pulled(tiles_flag, 0, None, x, dx, dy, dz)
                moved = pulled(tiles, step, d, x, dx, dy, dz)
                state[d, x] = jnp.where(solid == 1.0, post[OPPOSITE[d], x], moved)
        if not last:
            velocity_tables()
        for copy in copies:
            copy.wait_send()

    state_copy = pltpu.make_async_copy(state, pop_out, out_sem.at[1])
    state_copy.start()
    each_peer(lambda peer: copy_a(peer, gx).wait_send())
    each_peer(lambda peer: copy_b(peer, gx).wait_send())
    each_peer(lambda peer: copy_r(peer, gx).wait_send())
    force_copy.wait()
    state_copy.wait()


def body(
    populations,
    flags,
    block_tile,
    marker_cell,
    marker_frac,
    marker_live,
    marker_target,
    marker_force,
):
    n_gx = lax.axis_size("gx")
    n_gy = lax.axis_size("gy")
    blocks, markers = marker_cell.shape
    width = n_gx * SLOT * markers
    f32, bf16, i32 = jnp.float32, jnp.bfloat16, jnp.int32
    dma = pltpu.SemaphoreType.DMA
    vmem = pltpu.VMEM
    anywhere = pl.BlockSpec(memory_space=pl.ANY)
    return pl.pallas_call(
        functools.partial(kernel, n_gx, n_gy),
        out_shape=(
            jax.ShapeDtypeStruct(populations.shape, f32),
            jax.ShapeDtypeStruct(marker_force.shape, f32),
        ),
        in_specs=[anywhere] * 8,
        out_specs=(anywhere, anywhere),
        scratch_shapes=[
            vmem(populations.shape, f32),
            vmem(populations.shape, f32),
            vmem(flags.shape, i32),
            pltpu.SMEM(block_tile.shape, i32),
            vmem(marker_cell.shape, i32),
            vmem(marker_frac.shape, f32),
            vmem(marker_live.shape, i32),
            vmem(marker_target.shape, f32),
            vmem(marker_force.shape, f32),
            vmem((n_gx, 8, markers), f32),
            vmem((n_gx, 8, markers), f32),
            vmem((n_gx, SLOT, 8, markers), f32),
            vmem((n_gx, SLOT, 8, markers), f32),
            vmem((n_gx, 8, markers), f32),
            vmem((n_gx, 8, markers), f32),
            vmem((n_gx, 8, markers), f32),
            vmem((2 * NZ, width), bf16),
            vmem((COLS, width), f32),
            vmem((6 * COLS, width), bf16),
            vmem((6 * COLS, 2 * NZ), bf16),
            vmem((3, CX, CY, NZ), f32),
            vmem((STEPS, 2, 6, CY, NZ), f32),
            vmem((STEPS, 2, 6, CY, NZ), f32),
            vmem((STEPS, 2, 24, NZ), f32),
            vmem((STEPS, 2, 24, NZ), f32),
            vmem((STEPS, 4, 8, NZ), f32),
            vmem((STEPS, 4, 8, NZ), f32),
            vmem(marker_force.shape, f32),
            dma((8,)),
            dma((2,)),
            dma((n_gx,)),
            dma((n_gx,)),
            dma((n_gx,)),
            dma((n_gx,)),
            dma((n_gx,)),
            dma((n_gx,)),
            dma((STEPS, 8)),
            dma((STEPS, 8)),
        ],
        compiler_params=pltpu.CompilerParams(
            collective_id=0,
            has_side_effects=True,
            vmem_limit_bytes=32 * 1024 * 1024,
        ),
    )(
        populations,
        flags,
        block_tile,
        marker_cell,
        marker_frac,
        marker_live,
        marker_target,
        marker_force,
    )


def solution(mesh):
    in_specs = (
        P(None, "gx", "gy", None),
        P("gx", "gy", None),
        P(("gx", "gy"), None),
        P(("gx", "gy"), None),
        P(("gx", "gy"), None, None),
        P(("gx", "gy"), None),
        P(("gx", "gy"), None, None),
        P(("gx", "gy"), None, None),
    )
    out_specs = (P(None, "gx", "gy", None), P(("gx", "gy"), None, None))
    return jax.shard_map(body, mesh=mesh, in_specs=in_specs, out_specs=out_specs, check_vma=False)
```

time: 169 us -> 45.3 us (0.27)
  the two profiles are of different devices: /device:TPU:7 before, /device:TPU:1 now
where the time goes in v1:
time: 45.3 us; the launch traced here: 45 us
  Pallas kernels  39.1 us (86%)
  local copies, waits for them, and re-layouts  5.24 us (12%)
  between operations  0.67 us (1%)
    pallas_call x1, Pallas kernels, body(): pl.pallas_call(functools.partial(kernel, n_gx, n_gy), out_shape=(jax.Shap...  39.1 us
    unnamed x17, local copies, waits for them, and re-layouts  4.63 us

profile of v1, /device:TPU:1, one launch (start us, length us, event | category | flops | bytes accessed | tf_op | source)
XLA Modules:
  0.0 45.0 jit_solution(15579008862203856415)
XLA Ops:
  0.6 0.7 %copy.10.tile_hbm = s32[16,1]{1,0:T(8,128)S(1)} copy(s32[16,1]{0,1:T(1,128)} %param.10) | data formatting | bytes 128 | tf_op args[2]
  1.4 0.0 copy-start.4
  1.4 0.8 %copy.11.frac_hbm = f32[16,3,128]{2,1,0:T(4,128)S(1)} copy(f32[16,3,128]{2,0,1:T(8,128)} %param.12) | data formatting | bytes 49152 | tf_op args[4]
  2.1 0.0 copy-done.4
  2.1 0.0 copy-start.5
  2.2 0.7 %copy-done.5 = f32[16,3,128]{2,0,1:T(8,128)S(1)} copy-done((f32[16,3,128]{2,0,1:T(8,128)S(1)}, f32[16,3,128]{2,0,1:T(8,128)}, u32[]{:S(2)}) %copy-start.5) | copy-done | bytes 24600
  2.9 0.0 copy-start.1
  2.9 0.0 copy-start.2
  2.9 0.0 copy-start.3
  2.9 0.7 %copy-done.1 = s32[4,8,128]{2,1,0:T(8,128)S(1)} copy-done((s32[4,8,128]{2,1,0:T(8,128)S(1)}, s32[4,8,128]{2,1,0:T(8,128)}, u32[]{:S(2)}) %copy-start.1) | copy-done | bytes 16408
  3.6 0.0 copy-done.2
  3.6 0.0 copy-done.3
  3.6 0.0 copy-start
  3.6 1.0 %copy-done = f32[19,4,8,128]{3,2,1,0:T(8,128)S(1)} copy-done((f32[19,4,8,128]{3,2,1,0:T(8,128)S(1)}, f32[19,4,8,128]{3,2,1,0:T(8,128)}, u32[]{:S(2)}) %copy-start) | copy-done | bytes 311320
  4.6 39.1 %shard_map.95 = (f32[19,4,8,128]{3,2,1,0:T(8,128)S(1)}, f32[16,3,128]{2,1,0:T(4,128)S(1)}) custom-call(f32[19,4,8,128]{3,2,1,0:T(8,128)S(1)} %copy-done, s32[4,8,128]{2,1,0:T(8,128)S(1)} %copy-done.1, s32[16,1]{1,0:T(8,128)S(1)} %copy.10.tile_hbm, s32[16,128]{1,0:T(8,128)S(1)} %copy-done.2, f32[16,3,128]{2,1,0:T(4,128)S(1)} %copy.11.frac_hbm, ...), custom_call_target="tpu_custom_call" | custom-call | tf_op jit(solution)/shard_map/pallas_call | solution.py:542
  43.7 0.6 %copy.14 = f32[16,3,128]{2,0,1:T(8,128)} copy(f32[16,3,128]{2,1,0:T(4,128)S(1)} %get-tuple-element.3) | data formatting | bytes 49152 | tf_op jit(solution)/shard_map/pallas_call | solution.py:542
  44.3 0.7 %copy.16 = f32[19,4,8,128]{3,2,1,0:T(8,128)} copy(f32[19,4,8,128]{3,2,1,0:T(8,128)S(1)} %get-tuple-element.6) | data formatting | bytes 622592
  (2 shorter events, 0.0 us)
Async XLA Ops:
  1.4 0.8 %copy-start.4 = (f32[16,3,128]{2,0,1:T(8,128)S(1)}, f32[16,3,128]{2,0,1:T(8,128)}, u32[]{:S(2)}) copy-start(f32[16,3,128]{2,0,1:T(8,128)} %param.14) | copy-start | bytes 73732
  2.1 0.7 %copy-start.5 = (f32[16,3,128]{2,0,1:T(8,128)S(1)}, f32[16,3,128]{2,0,1:T(8,128)}, u32[]{:S(2)}) copy-start(f32[16,3,128]{2,0,1:T(8,128)} %param.15) | copy-start | bytes 73732
  2.9 0.7 %copy-start.1 = (s32[4,8,128]{2,1,0:T(8,128)S(1)}, s32[4,8,128]{2,1,0:T(8,128)}, u32[]{:S(2)}) copy-start(s32[4,8,128]{2,1,0:T(8,128)} %flags_hbm.1) | copy-start | bytes 49156
  2.9 0.7 %copy-start.2 = (s32[16,128]{1,0:T(8,128)S(1)}, s32[16,128]{1,0:T(8,128)}, u32[]{:S(2)}) copy-start(s32[16,128]{1,0:T(8,128)} %cell_hbm.1) | copy-start | bytes 24580
  2.9 0.7 %copy-start.3 = (s32[16,128]{1,0:T(8,128)S(1)}, s32[16,128]{1,0:T(8,128)}, u32[]{:S(2)}) copy-start(s32[16,128]{1,0:T(8,128)} %live_hbm.1) | copy-start | bytes 24580
  3.6 1.0 %copy-start = (f32[19,4,8,128]{3,2,1,0:T(8,128)S(1)}, f32[19,4,8,128]{3,2,1,0:T(8,128)}, u32[]{:S(2)}) copy-start(f32[19,4,8,128]{3,2,1,0:T(8,128)} %pop_hbm.1) | copy-start | bytes 933892

commit v2 on v1

v2 whole, which is shorter than its diff:
```python
import functools

import jax
import jax.numpy as jnp
from jax import lax
from jax.experimental import pallas as pl
from jax.experimental.pallas import tpu as pltpu
from jax.sharding import PartitionSpec as P

STEPS = 2
SLOT = 2
MESH = pl.DeviceIdType.MESH

VELOCITIES = (
    (0, 0, 0),
    (1, 0, 0),
    (-1, 0, 0),
    (0, 1, 0),
    (0, -1, 0),
    (0, 0, 1),
    (0, 0, -1),
    (1, 1, 0),
    (-1, -1, 0),
    (1, -1, 0),
    (-1, 1, 0),
    (1, 0, 1),
    (-1, 0, -1),
    (1, 0, -1),
    (-1, 0, 1),
    (0, 1, 1),
    (0, -1, -1),
    (0, 1, -1),
    (0, -1, 1),
)
OPPOSITE = (0, 2, 1, 4, 3, 6, 5, 8, 7, 10, 9, 12, 11, 14, 13, 16, 15, 18, 17)
WEIGHTS = (1.0 / 3.0,) + (1.0 / 18.0,) * 6 + (1.0 / 36.0,) * 12
OMEGA = 1.25

EAST = tuple(d for d in range(19) if VELOCITIES[d][0] == 1)
WEST = tuple(d for d in range(19) if VELOCITIES[d][0] == -1)
NORTH = tuple(d for d in range(19) if VELOCITIES[d][1] == 1)
SOUTH = tuple(d for d in range(19) if VELOCITIES[d][1] == -1)
XDIRS = {1: EAST, -1: WEST}
YDIRS = {1: NORTH, -1: SOUTH}
CORNERS = ((1, 1), (-1, -1), (1, -1), (-1, 1))
CORNER_DIR = {(1, 1): 7, (-1, -1): 8, (1, -1): 9, (-1, 1): 10}

NEIGHBOURS = ((1, 0), (-1, 0), (0, 1), (0, -1)) + CORNERS
GROUPS = 4

CX, CY, NZ = 4, 8, 128
COLS = CX * CY


def dot_product(direction, vector):
    total = None
    for component in range(3):
        factor = VELOCITIES[direction][component]
        if factor != 0:
            term = vector[component] if factor == 1 else -vector[component]
            total = term if total is None else total + term
    return total


def moments(f):
    density = f[0]
    for d in range(1, 19):
        density = density + f[d]
    parts = []
    for component in range(3):
        plus = minus = None
        for d in range(19):
            factor = VELOCITIES[d][component]
            if factor == 1:
                plus = f[d] if plus is None else plus + f[d]
            elif factor == -1:
                minus = f[d] if minus is None else minus + f[d]
        parts.append(plus - minus)
    inverse = 1.0 / density
    return density, inverse, [part * inverse for part in parts]


def collide(f, density, inverse, velocity, field):
    half = 0.5 * inverse
    shifted = [velocity[c] + field[c] * half for c in range(3)]
    squared = shifted[0] * shifted[0] + shifted[1] * shifted[1] + shifted[2] * shifted[2]
    power = shifted[0] * field[0] + shifted[1] * field[1] + shifted[2] * field[2]
    gain = 1.0 - 0.5 * OMEGA
    scaled = OMEGA * density
    base = scaled * (1.0 - 1.5 * squared) - (3.0 * gain) * power
    curved = 4.5 * scaled
    sloped = 3.0 * scaled
    post = [None] * 19
    post[0] = (1.0 - OMEGA) * f[0] + WEIGHTS[0] * base
    for d in range(1, 19, 2):
        s = dot_product(d, shifted)
        g = dot_product(d, field)
        even = base + s * (curved * s + (9.0 * gain) * g)
        odd = sloped * s + (3.0 * gain) * g
        post[d] = (1.0 - OMEGA) * f[d] + WEIGHTS[d] * (even + odd)
        post[d + 1] = (1.0 - OMEGA) * f[d + 1] + WEIGHTS[d] * (even - odd)
    return post


def offsets(count):
    order = [0]
    for step in range(1, count // 2 + 1):
        order.append(step)
        if 2 * step != count:
            order.append(-step)
    return order


def kernel(
    n_gx,
    n_gy,
    pop_hbm,
    flags_hbm,
    tile_hbm,
    cell_hbm,
    frac_hbm,
    live_hbm,
    target_hbm,
    force_hbm,
    pop_out,
    force_out,
    state,
    post,
    moment_v,
    flags_v,
    tile_s,
    cell_v,
    frac_v,
    live_v,
    target_v,
    force_v,
    push_v,
    pull_v,
    send_a,
    recv_a,
    send_b,
    recv_b,
    send_c,
    recv_c,
    send_r,
    recv_r,
    force_now,
    sample_v,
    z_table,
    zt_table,
    c_table,
    s_table,
    v_table,
    solid_v,
    solid_row,
    back_row,
    flag_send,
    flag_recv,
    face_send,
    face_recv,
    edge_send,
    edge_recv,
    corner_send,
    corner_recv,
    in_sem,
    a_send_sem,
    a_recv_sem,
    b_send_sem,
    b_recv_sem,
    c_send_sem,
    c_recv_sem,
    r_send_sem,
    r_recv_sem,
    f_send_sem,
    f_recv_sem,
    h_send_sem,
    h_recv_sem,
):
    gx = lax.axis_index("gx")
    gy = lax.axis_index("gy")
    blocks = cell_v.shape[0]
    near = offsets(n_gx)
    place_of = {off % n_gx: n for n, off in enumerate(near)}
    far_first = list(range(n_gx - 1, 0, -1))

    def around(position, shift, count):
        return lax.rem(position + (shift + count), count)

    def device(dx, dy):
        if dy == 0:
            return {"gx": around(gx, dx, n_gx)}
        if dx == 0:
            return {"gy": around(gy, dy, n_gy)}
        return {"gx": around(gx, dx, n_gx), "gy": around(gy, dy, n_gy)}

    barrier = pltpu.get_barrier_semaphore()
    for n in far_first:
        pl.semaphore_signal(barrier, inc=1, device_id=device(near[n], 0), device_id_type=MESH)
    for dx, dy in NEIGHBOURS:
        if dy != 0:
            pl.semaphore_signal(barrier, inc=1, device_id=device(dx, dy), device_id_type=MESH)

    in_pairs = (
        (tile_hbm, tile_s),
        (cell_hbm, cell_v),
        (frac_hbm, frac_v),
        (live_hbm, live_v),
        (target_hbm, target_v),
        (force_hbm, force_v),
        (pop_hbm, state),
        (flags_hbm, flags_v),
    )
    loads = [
        pltpu.make_async_copy(src, dst, in_sem.at[i]) for i, (src, dst) in enumerate(in_pairs)
    ]
    for load in loads:
        load.start()
    for load in loads[:6]:
        load.wait()

    alive = live_v[...].astype(jnp.float32)
    for c in range(3):
        pull_v[c] = alive * target_v[c]
        push_v[c] = alive * (force_v[c] + target_v[c])

    def pack(t, carry):
        first = jnp.int32(-1)
        second = jnp.int32(-1)
        for b in range(blocks - 1, -1, -1):
            match = tile_s[0, b] == t
            second = jnp.where(match, first, second)
            first = jnp.where(match, jnp.int32(b), first)
        for s, index in enumerate((first, second)):
            valid = jnp.where(index >= 0, 1.0, 0.0)
            at = pl.ds(jnp.maximum(index, 0), 1)
            send_a[t, 4 * s : 4 * s + 1, :] = cell_v[at, :].astype(jnp.float32)
            for c in range(3):
                send_a[t, 4 * s + 1 + c : 4 * s + 2 + c, :] = frac_v[c, at, :]
                send_b[t, 4 * s + c : 4 * s + c + 1, :] = push_v[c, at, :] * valid
                send_c[t, 3 * s + c : 3 * s + c + 1, :] = pull_v[c, at, :] * valid
            send_b[t, 4 * s + 3 : 4 * s + 4, :] = live_v[at, :].astype(jnp.float32) * valid
        return carry

    lax.fori_loop(0, n_gx, pack, 0)
    recv_a[0] = send_a[gx]
    recv_b[0] = send_b[gx]
    recv_c[0] = send_c[gx]

    loads[7].wait()
    for number, (dx, dy) in enumerate(NEIGHBOURS):
        x = CX - 1 if dx == 1 else 0
        y = CY - 1 if dy == 1 else 0
        if dy == 0:
            flag_send[number] = flags_v[x].astype(jnp.float32)
        elif dx == 0:
            for x in range(CX):
                flag_send[number, x : x + 1, :] = flags_v[x, y : y + 1, :].astype(jnp.float32)
        else:
            flag_send[number, 0:1, :] = flags_v[x, y : y + 1, :].astype(jnp.float32)

    def peer_copy(send, recv, send_sem, recv_sem, rows=8):
        def copy(n):
            back = place_of[-near[n] % n_gx]
            return pltpu.make_async_remote_copy(
                src_ref=send.at[around(gx, near[n], n_gx), 0:rows],
                dst_ref=recv.at[back, 0:rows],
                send_sem=send_sem.at[n],
                recv_sem=recv_sem.at[back],
                device_id=device(near[n], 0),
                device_id_type=MESH,
            )

        return {n: copy(n) for n in far_first}

    def opposite(n):
        return place_of[-near[n] % n_gx]

    copies_a = peer_copy(send_a, recv_a, a_send_sem, a_recv_sem)
    copies_b = peer_copy(send_b, recv_b, b_send_sem, b_recv_sem)
    copies_c = peer_copy(send_c, recv_c, c_send_sem, c_recv_sem, 6)
    copies_r = {
        n: pltpu.make_async_remote_copy(
            src_ref=send_r.at[n, 0:6],
            dst_ref=recv_r.at[gx, 0:6],
            send_sem=r_send_sem.at[n],
            recv_sem=r_recv_sem.at[opposite(n)],
            device_id=device(near[n], 0),
            device_id_type=MESH,
        )
        for n in far_first
    }
    flag_rows = (CY, CY, CX, CX, 1, 1, 1, 1)
    copies_f = [
        pltpu.make_async_remote_copy(
            src_ref=flag_send.at[number, 0 : flag_rows[number]],
            dst_ref=flag_recv.at[number, 0 : flag_rows[number]],
            send_sem=f_send_sem.at[number],
            recv_sem=f_recv_sem.at[number],
            device_id=device(dx, dy),
            device_id_type=MESH,
        )
        for number, (dx, dy) in enumerate(NEIGHBOURS)
    ]

    pl.semaphore_wait(barrier, n_gx - 1 + 6)
    for n in far_first:
        copies_a[n].start()
    for n in far_first:
        copies_b[n].start()
    for copy in copies_f:
        copy.start()

    loads[6].wait()

    def velocity_tables(f):
        density, inverse, velocity = moments(f)
        moment_v[0] = density
        moment_v[1] = inverse
        for c in range(3):
            moment_v[2 + c] = velocity[c]
            rows = velocity[c].reshape(COLS, NZ)
            high = rows.astype(jnp.bfloat16)
            low = (rows - high.astype(jnp.float32)).astype(jnp.bfloat16)
            for half in range(2):
                v_table[c * COLS : (c + 1) * COLS, half * NZ : (half + 1) * NZ] = high
                v_table[(3 + c) * COLS : (4 + c) * COLS, half * NZ : (half + 1) * NZ] = low

    velocity_tables([state[d] for d in range(19)])

    y_rows = lax.broadcasted_iota(jnp.int32, (CY, NZ), 0)
    z_rows = lax.broadcasted_iota(jnp.int32, (16, NZ), 0)

    def build(n):
        for s in range(SLOT):
            begin = (n * SLOT + s) * NZ
            column = slice(begin, begin + NZ)
            cell = recv_a[n, 4 * s : 4 * s + 1, :].astype(jnp.int32)
            px = recv_a[n, 4 * s + 1 : 4 * s + 2, :]
            py = recv_a[n, 4 * s + 2 : 4 * s + 3, :]
            pz = recv_a[n, 4 * s + 3 : 4 * s + 4, :]
            i = lax.shift_right_logical(cell, 10)
            j = lax.shift_right_logical(cell, 7) & 7
            k = cell & 127
            wide = (CY, NZ)
            jw = jnp.broadcast_to(j, wide)
            pyw = jnp.broadcast_to(py, wide)
            wy = jnp.where(y_rows == jw, 1.0 - pyw, jnp.where(y_rows == jw + 1, pyw, 0.0))
            for x in range(CX):
                wx = jnp.where(i == x, 1.0 - px, jnp.where(i == x - 1, px, 0.0))
                c_table[x * CY : (x + 1) * CY, column] = jnp.broadcast_to(wx, wide) * wy
            tall = (16, NZ)
            kw = jnp.broadcast_to(k, tall)
            upper = jnp.broadcast_to(pz, tall)
            lower = 1.0 - upper
            upper_high = upper.astype(jnp.bfloat16)
            lower_high = lower.astype(jnp.bfloat16)
            upper_low = (upper - upper_high.astype(jnp.float32)).astype(jnp.bfloat16)
            lower_low = (lower - lower_high.astype(jnp.float32)).astype(jnp.bfloat16)
            k16 = kw.astype(jnp.bfloat16)
            none = jnp.zeros(tall, jnp.bfloat16)
            for chunk in range(NZ // 16):
                here = (z_rows + 16 * chunk).astype(jnp.bfloat16)
                below = (z_rows + (16 * chunk - 1)).astype(jnp.bfloat16)
                is_low = here == k16
                is_up = below == k16
                z_table[16 * chunk : 16 * chunk + 16, column] = jnp.where(
                    is_low, lower_high, jnp.where(is_up, upper_high, none)
                )
                z_table[NZ + 16 * chunk : NZ + 16 * chunk + 16, column] = jnp.where(
                    is_low, lower_low, jnp.where(is_up, upper_low, none)
                )

    def sample(n):
        wide = slice(n * SLOT * NZ, (n + 1) * SLOT * NZ)
        picked = jnp.dot(v_table[...], z_table[:, wide], preferred_element_type=jnp.float32)
        weights = c_table[:, wide]
        for c in range(3):
            both = (
                picked[c * COLS : (c + 1) * COLS] + picked[(3 + c) * COLS : (4 + c) * COLS]
            ) * weights
            sampled = jnp.sum(both, axis=0, keepdims=True)
            for s in range(SLOT):
                sample_v[n, 3 * s + c : 3 * s + c + 1, :] = sampled[:, s * NZ : (s + 1) * NZ]

    def push(n, step):
        for s in range(SLOT):
            rows = slice(3 * s, 3 * s + 3)
            column = slice((n * SLOT + s) * NZ, (n * SLOT + s + 1) * NZ)
            live = recv_b[n, 4 * s + 3 : 4 * s + 4, :]
            if step == 0:
                before = recv_b[n, 4 * s : 4 * s + 3, :]
            else:
                before = force_now[n, rows, :] + recv_c[n, rows, :]
            pushed = before - live * sample_v[n, rows, :]
            into = send_r if step == STEPS - 1 else force_now
            into[n, rows, :] = pushed
            for c in range(3):
                spread_row = c_table[:, column] * pushed[c : c + 1]
                high = spread_row.astype(jnp.bfloat16)
                low = (spread_row - high.astype(jnp.float32)).astype(jnp.bfloat16)
                s_table[c * COLS : (c + 1) * COLS, column] = high
                s_table[(3 + c) * COLS : (4 + c) * COLS, column] = low

    def spread(members, step):
        wide = slice(members[0] * SLOT * NZ, (members[-1] + 1) * SLOT * NZ)
        if step > 0:
            return jnp.dot(
                s_table[:, wide], zt_table[wide, :], preferred_element_type=jnp.float32
            )
        return lax.dot_general(
            s_table[:, wide],
            z_table[:, wide],
            (((1,), (1,)), ((), ())),
            preferred_element_type=jnp.float32,
        )

    def turn_table():
        for block in range(n_gx * SLOT):
            for half in range(2):
                zt_table[block * NZ : (block + 1) * NZ, half * NZ : (half + 1) * NZ] = z_table[
                    half * NZ : (half + 1) * NZ, block * NZ : (block + 1) * NZ
                ].T

    def rim_copies(step):
        def copy(number, src, dst):
            return pltpu.make_async_remote_copy(
                src_ref=src,
                dst_ref=dst,
                send_sem=h_send_sem.at[step, number],
                recv_sem=h_recv_sem.at[step, number],
                device_id=device(*NEIGHBOURS[number]),
                device_id_type=MESH,
            )

        out = []
        for number in range(8):
            if number < 2:
                out.append(
                    copy(number, face_send.at[step, number], face_recv.at[step, number])
                )
            elif number < 4:
                out.append(
                    copy(
                        number,
                        edge_send.at[step, number - 2, 0:20],
                        edge_recv.at[step, number - 2, 0:20],
                    )
                )
            else:
                out.append(
                    copy(
                        number,
                        corner_send.at[step, number - 4, 0:1],
                        corner_recv.at[step, number - 4, 0:1],
                    )
                )
        return out

    def shifted(tile, dy, dz):
        if dy != 0:
            tile = pltpu.roll(tile, 1 if dy == 1 else CY - 1, 0)
        if dz != 0:
            tile = pltpu.roll(tile, 1 if dz == 1 else NZ - 1, 1)
        return tile

    def solid_masks():
        tiles = [flags_v[x].astype(jnp.float32) for x in range(CX)]
        sublane = lax.broadcasted_iota(jnp.int32, (CY, NZ), 0)
        for d in range(1, 19):
            dx, dy, dz = VELOCITIES[d]
            for x in range(CX):
                from_x = x - dx
                outside = from_x < 0 or from_x >= CX
                if outside:
                    tile = flag_recv[NEIGHBOURS.index((dx, 0))]
                else:
                    tile = tiles[from_x]
                if dy != 0:
                    if outside:
                        row = flag_recv[NEIGHBOURS.index((dx, dy)), 0:1, :]
                    else:
                        row = flag_recv[NEIGHBOURS.index((0, dy)), from_x : from_x + 1, :]
                    edge = 0 if dy == 1 else CY - 1
                    tile = jnp.where(
                        sublane == edge, jnp.broadcast_to(row, (CY, NZ)), shifted(tile, dy, 0)
                    )
                solid_v[d, x] = shifted(tile, 0, dz)
        for side, sy in enumerate((1, -1)):
            y = 0 if sy == 1 else CY - 1
            solid_row[side] = jnp.zeros((24, NZ), jnp.float32)
            back_row[side] = jnp.zeros((24, NZ), jnp.float32)
            for place, d in enumerate(YDIRS[sy]):
                for from_x in range(CX):
                    x = from_x + VELOCITIES[d][0]
                    if 0 <= x < CX:
                        row = 4 * place + from_x
                        solid_row[side, row : row + 1, :] = solid_v[d, x, y : y + 1, :]

    def stream_inside(into):
        into[0] = post[0]
        for d in range(1, 19):
            dx, dy, dz = VELOCITIES[d]
            for x in range(CX):
                if 0 <= x - dx < CX:
                    moved = shifted(post[d, x - dx], dy, dz)
                    into[d, x] = jnp.where(solid_v[d, x] == 1.0, post[OPPOSITE[d], x], moved)
        for side, sy in enumerate((1, -1)):
            y = 0 if sy == 1 else CY - 1
            for place, d in enumerate(YDIRS[sy]):
                for from_x in range(CX):
                    x = from_x + VELOCITIES[d][0]
                    if 0 <= x < CX:
                        row = 4 * place + from_x
                        back_row[side, row : row + 1, :] = post[OPPOSITE[d], x, y : y + 1, :]

    def stream_edge(into, step, side):
        sy = (1, -1)[side]
        y = 0 if sy == 1 else CY - 1
        dirs = YDIRS[sy]
        half = lax.broadcasted_iota(jnp.int32, (8, NZ), 0) < 4
        parts = [edge_recv[step, side, 8 * p : 8 * p + (4 if p == 2 else 8), :] for p in range(3)]
        parts[1] = jnp.where(half, parts[1], shifted(parts[1], 0, VELOCITIES[dirs[3]][2]))
        parts[2] = shifted(parts[2], 0, VELOCITIES[dirs[4]][2])
        parts = [
            jnp.where(
                solid_row[side, 8 * p : 8 * p + parts[p].shape[0], :] == 1.0,
                back_row[side, 8 * p : 8 * p + parts[p].shape[0], :],
                parts[p],
            )
            for p in range(3)
        ]
        for place, d in enumerate(dirs):
            for from_x in range(CX):
                x = from_x + VELOCITIES[d][0]
                if 0 <= x < CX:
                    row = 4 * place + from_x
                    into[d, x, y : y + 1, :] = parts[row // 8][row % 8 : row % 8 + 1, :]

    def stream_face(into, step, side):
        sx = (1, -1)[side]
        x = 0 if sx == 1 else CX - 1
        for place, d in enumerate(XDIRS[sx]):
            _, dy, dz = VELOCITIES[d]
            moved = shifted(face_recv[step, side, place], dy, dz)
            into[d, x] = jnp.where(solid_v[d, x] == 1.0, post[OPPOSITE[d], x], moved)

    def stream_corner(into, step, corner):
        sx, sy = CORNERS[corner]
        d = CORNER_DIR[sx, sy]
        x = 0 if sx == 1 else CX - 1
        y = slice(0, 1) if sy == 1 else slice(CY - 1, CY)
        into[d, x, y, :] = jnp.where(
            solid_v[d, x, y, :] == 1.0,
            post[OPPOSITE[d], x, y, :],
            corner_recv[step, corner, 0:1, :],
        )

    per = n_gx // GROUPS
    groups = [list(range(g * per, (g + 1) * per)) for g in range(GROUPS)]
    all_rims = []
    for step in range(STEPS):
        last = step == STEPS - 1
        total = None
        if step == 0:
            for members in groups:
                for n in members:
                    if n > 0:
                        copies_a[opposite(n)].wait_recv()
                for n in members:
                    build(n)
                for n in members:
                    sample(n)
        for members in groups:
            if step == 0:
                for n in members:
                    if n > 0:
                        copies_b[opposite(n)].wait_recv()
            else:
                for n in members:
                    sample(n)
                if members is groups[0]:
                    for n in far_first:
                        copies_c[opposite(n)].wait_recv()
            for n in members:
                push(n, step)
            if members is groups[-1]:
                if step == 0:
                    for n in far_first:
                        copies_c[n].start()
                if last:
                    recv_r[gx] = send_r[0]
                    for n in far_first:
                        copies_r[n].start()
            part = spread(members, step)
            total = part if total is None else total + part
        field = (total[: 3 * COLS, :NZ] + total[3 * COLS :, :NZ]) + (
            total[: 3 * COLS, NZ:] + total[3 * COLS :, NZ:]
        )
        field = field.reshape(3, CX, CY, NZ)
        f = [state[d] for d in range(19)]
        after = collide(
            f,
            moment_v[0],
            moment_v[1],
            [moment_v[2 + c] for c in range(3)],
            [field[c] for c in range(3)],
        )
        copies = rim_copies(step)
        for corner, (sx, sy) in enumerate(CORNERS):
            x = CX - 1 if sx == 1 else 0
            y = CY - 1 if sy == 1 else 0
            corner_send[step, corner, 0:1, :] = after[CORNER_DIR[sx, sy]][x, y : y + 1, :]
        for side, sx in enumerate((1, -1)):
            for place, d in enumerate(XDIRS[sx]):
                face_send[step, side, place] = after[d][CX - 1 if sx == 1 else 0]
        for side, sy in enumerate((1, -1)):
            y = CY - 1 if sy == 1 else 0
            for place, d in enumerate(YDIRS[sy]):
                for x in range(CX):
                    row = 4 * place + x
                    edge_send[step, side, row : row + 1, :] = after[d][x, y : y + 1, :]
        for number in (4, 5, 6, 7, 0, 1, 2, 3):
            copies[number].start()
        for d in range(19):
            post[d] = after[d]
        into = pop_out if last else state
        if step == 0:
            for copy in copies_f:
                copy.wait_recv()
            turn_table()
            solid_masks()
        stream_inside(into)
        for side in range(2):
            copies[2 + side].wait_recv()
            stream_edge(into, step, side)
        if last:
            for n in far_first:
                copies_r[opposite(n)].wait_recv()
            for b in range(blocks):
                tile = tile_s[0, b]
                rank = jnp.int32(0)
                for other in range(b):
                    rank = rank + jnp.where(tile_s[0, other] == tile, 1, 0)
                half = jnp.where(rank == 0, recv_r[tile, 0:3, :], recv_r[tile, 3:6, :])
                for c in range(3):
                    push_v[c, b : b + 1, :] = half[c : c + 1]
            keep = live_v[...] == 1
            for c in range(3):
                force_out[c] = jnp.where(keep, push_v[c], force_v[c])
        for side in range(2):
            copies[side].wait_recv()
            stream_face(into, step, side)
        for corner in range(4):
            copies[4 + corner].wait_recv()
            stream_corner(into, step, corner)
        if not last:
            velocity_tables([state[d] for d in range(19)])
        all_rims += copies

    for group in (copies_a, copies_b, copies_c, copies_r):
        for n in far_first:
            group[n].wait_send()
    for copy in copies_f + all_rims:
        copy.wait_send()


def deliver(state, force, state_out, force_out, sem):
    copies = [
        pltpu.make_async_copy(state, state_out, sem.at[0]),
        pltpu.make_async_copy(force, force_out, sem.at[1]),
    ]
    for copy in copies:
        copy.start()
    for copy in copies:
        copy.wait()


def body(
    populations,
    flags,
    block_tile,
    marker_cell,
    marker_frac,
    marker_live,
    marker_target,
    marker_force,
):
    n_gx = lax.axis_size("gx")
    n_gy = lax.axis_size("gy")
    blocks, markers = marker_cell.shape
    width = n_gx * SLOT * markers
    marker_rows = (3, blocks, markers)
    packed = (n_gx, 8, markers)
    f32, bf16, i32 = jnp.float32, jnp.bfloat16, jnp.int32
    dma = pltpu.SemaphoreType.DMA
    vmem = pltpu.VMEM
    in_hbm = functools.partial(pltpu.with_memory_space_constraint, memory_space=pltpu.HBM)
    in_vmem = functools.partial(pltpu.with_memory_space_constraint, memory_space=pltpu.VMEM)
    anywhere = pl.BlockSpec(memory_space=pl.ANY)
    inside = pl.BlockSpec(memory_space=pltpu.VMEM)
    state, force = pl.pallas_call(
        functools.partial(kernel, n_gx, n_gy),
        out_shape=(vmem(populations.shape, f32), vmem(marker_rows, f32)),
        in_specs=[anywhere] * 8,
        out_specs=(inside, inside),
        scratch_shapes=[
            vmem(populations.shape, f32),
            vmem(populations.shape, f32),
            vmem((5, CX, CY, NZ), f32),
            vmem(flags.shape, i32),
            pltpu.SMEM((1, blocks), i32),
            vmem(marker_cell.shape, i32),
            vmem(marker_rows, f32),
            vmem(marker_live.shape, i32),
            vmem(marker_rows, f32),
            vmem(marker_rows, f32),
            vmem(marker_rows, f32),
            vmem(marker_rows, f32),
        ]
        + [vmem(packed, f32)] * 10
        + [
            vmem((2 * NZ, width), bf16),
            vmem((width, 2 * NZ), bf16),
            vmem((COLS, width), f32),
            vmem((6 * COLS, width), bf16),
            vmem((6 * COLS, 2 * NZ), bf16),
            vmem(populations.shape, f32),
            vmem((2, 24, NZ), f32),
            vmem((2, 24, NZ), f32),
            vmem((8, CY, NZ), f32),
            vmem((8, CY, NZ), f32),
            vmem((STEPS, 2, 5, CY, NZ), f32),
            vmem((STEPS, 2, 5, CY, NZ), f32),
            vmem((STEPS, 2, 24, NZ), f32),
            vmem((STEPS, 2, 24, NZ), f32),
            vmem((STEPS, 4, 8, NZ), f32),
            vmem((STEPS, 4, 8, NZ), f32),
            dma((8,)),
        ]
        + [dma((n_gx,))] * 8
        + [dma((8,))] * 2
        + [dma((STEPS, 8))] * 2,
        compiler_params=pltpu.CompilerParams(
            collective_id=0,
            has_side_effects=True,
            vmem_limit_bytes=32 * 1024 * 1024,
        ),
    )(
        in_hbm(populations),
        in_hbm(flags),
        in_hbm(block_tile.T),
        in_hbm(marker_cell),
        in_hbm(marker_frac.transpose(1, 0, 2)),
        in_hbm(marker_live),
        in_hbm(marker_target.transpose(1, 0, 2)),
        in_hbm(marker_force.transpose(1, 0, 2)),
    )
    state, force = pl.pallas_call(
        deliver,
        out_shape=(
            jax.ShapeDtypeStruct(populations.shape, f32),
            jax.ShapeDtypeStruct(marker_rows, f32),
        ),
        in_specs=[inside] * 2,
        out_specs=(anywhere, anywhere),
        scratch_shapes=[dma((2,))],
    )(in_vmem(state), in_vmem(force))
    return state, force.transpose(1, 0, 2)


def solution(mesh):
    in_specs = (
        P(None, "gx", "gy", None),
        P("gx", "gy", None),
        P(("gx", "gy"), None),
        P(("gx", "gy"), None),
        P(("gx", "gy"), None, None),
        P(("gx", "gy"), None),
        P(("gx", "gy"), None, None),
        P(("gx", "gy"), None, None),
    )
    out_specs = (P(None, "gx", "gy", None), P(("gx", "gy"), None, None))
    return jax.shard_map(body, mesh=mesh, in_specs=in_specs, out_specs=out_specs, check_vma=False)
```

time: 45.3 us -> 33.5 us (0.74)
  Pallas kernels: 39.1 us -> 32.8 us
  local copies, waits for them, and re-layouts: 5.24 us -> 0 us
    pallas_call x1 -> x2, Pallas kernels: 39.1 us -> 32.8 us  [the longest x1 32.1 us: body(): pl.pallas_call(functools.partial(kernel, n_gx, n_gy), out_shape=(vmem(pop...]
    unnamed x17 -> x0, local copies, waits for them, and re-layouts: 4.63 us -> none
    pallas_call x1 -> x0, local copies, waits for them, and re-layouts: 0.61 us -> none  [body(): pl.pallas_call(functools.partial(kernel, n_gx, n_gy), out_shape=(jax.Shap...]
where the time goes in v2:
time: 33.5 us; the launch traced here: 33.4 us
  Pallas kernels  32.8 us (98%)
  between operations  0.64 us (2%)
    pallas_call x1, Pallas kernels, body(): pl.pallas_call(functools.partial(kernel, n_gx, n_gy), out_shape=(vmem(pop...  32.1 us
    pallas_call x1, Pallas kernels, body(): pl.pallas_call(deliver, out_shape=(jax.ShapeDtypeStruct(populations.shape...  0.74 us

profile of v2, /device:TPU:1, one launch (start us, length us, event | category | flops | bytes accessed | tf_op | source)
XLA Modules:
  0.0 33.4 jit_solution(5237903933607792010)
XLA Ops:
  0.6 32.1 %shard_map.95 = (f32[19,4,8,128]{3,2,1,0:T(8,128)S(1)}, f32[3,16,128]{2,1,0:T(8,128)S(1)}) custom-call(f32[19,4,8,128]{3,2,1,0:T(8,128)} %pop_hbm.1, s32[4,8,128]{2,1,0:T(8,128)} %flags_hbm.1, s32[1,16]{1,0:T(1,128)} %bitcast.8, s32[16,128]{1,0:T(8,128)} %cell_hbm.1, f32[3,16,128]{2,1,0:T(8,128)} %bitcast.5, s32[16,128]{1,0:T(8,128)} %live_hbm.1, ...), custom_call_target="tpu_custom_call" | custom-call | tf_op jit(solution)/shard_map/pallas_call | solution.py:701
  32.7 0.7 %shard_map.96 = (f32[19,4,8,128]{3,2,1,0:T(8,128)}, f32[3,16,128]{2,1,0:T(8,128)}) custom-call(f32[19,4,8,128]{3,2,1,0:T(8,128)S(1)} %get-tuple-element.6.state, f32[3,16,128]{2,1,0:T(8,128)S(1)} %get-tuple-element.7.force), custom_call_target="tpu_custom_call" | custom-call | tf_op jit(solution)/shard_map/pallas_call | solution.py:758

commit v3 on v2

--- a/solution.py
+++ b/solution.py
@@ -557,7 +557,7 @@
 
     per = n_gx // GROUPS
     groups = [list(range(g * per, (g + 1) * per)) for g in range(GROUPS)]
-    all_rims = []
+    rims = None
     for step in range(STEPS):
         last = step == STEPS - 1
         total = None
@@ -583,14 +583,9 @@
                         copies_c[opposite(n)].wait_recv()
             for n in members:
                 push(n, step)
-            if members is groups[-1]:
-                if step == 0:
-                    for n in far_first:
-                        copies_c[n].start()
-                if last:
-                    recv_r[gx] = send_r[0]
-                    for n in far_first:
-                        copies_r[n].start()
+            if step == 0 and members is groups[0]:
+                for n in far_first:
+                    copies_c[n].start()
             part = spread(members, step)
             total = part if total is None else total + part
         field = (total[: 3 * COLS, :NZ] + total[3 * COLS :, :NZ]) + (
@@ -621,46 +616,59 @@
                     edge_send[step, side, row : row + 1, :] = after[d][x, y : y + 1, :]
         for number in (4, 5, 6, 7, 0, 1, 2, 3):
             copies[number].start()
+        if last:
+            recv_r[gx] = send_r[0]
+            for n in far_first:
+                copies_r[n].start()
         for d in range(19):
             post[d] = after[d]
         into = pop_out if last else state
+        if last:
+            homes = [tile_s[0, b] for b in range(blocks)]
+            starts = []
+            for b in range(blocks):
+                rank = jnp.int32(0)
+                for other in range(b):
+                    rank = rank + jnp.where(homes[other] == homes[b], 3, 0)
+                starts.append(jnp.minimum(rank, 3))
         if step == 0:
             for copy in copies_f:
                 copy.wait_recv()
             turn_table()
             solid_masks()
         stream_inside(into)
+        if last:
+            for kind in (copies_a, copies_b, copies_c):
+                for n in far_first:
+                    kind[n].wait_send()
+            for copy in copies_f + rims:
+                copy.wait_send()
+        rims = copies
         for side in range(2):
             copies[2 + side].wait_recv()
             stream_edge(into, step, side)
-        if last:
-            for n in far_first:
-                copies_r[opposite(n)].wait_recv()
-            for b in range(blocks):
-                tile = tile_s[0, b]
-                rank = jnp.int32(0)
-                for other in range(b):
-                    rank = rank + jnp.where(tile_s[0, other] == tile, 1, 0)
-                half = jnp.where(rank == 0, recv_r[tile, 0:3, :], recv_r[tile, 3:6, :])
-                for c in range(3):
-                    push_v[c, b : b + 1, :] = half[c : c + 1]
-            keep = live_v[...] == 1
-            for c in range(3):
-                force_out[c] = jnp.where(keep, push_v[c], force_v[c])
         for side in range(2):
             copies[side].wait_recv()
             stream_face(into, step, side)
         for corner in range(4):
             copies[4 + corner].wait_recv()
             stream_corner(into, step, corner)
+        if last:
+            for n in far_first:
+                copies_r[opposite(n)].wait_recv()
+            for b in range(blocks):
+                half = recv_r[homes[b], pl.ds(starts[b], 3), :]
+                for c in range(3):
+                    push_v[c, b : b + 1, :] = half[c : c + 1]
+            keep = live_v[...] == 1
+            for c in range(3):
+                force_out[c] = jnp.where(keep, push_v[c], force_v[c])
         if not last:
             velocity_tables([state[d] for d in range(19)])
-        all_rims += copies
-
-    for group in (copies_a, copies_b, copies_c, copies_r):
-        for n in far_first:
-            group[n].wait_send()
-    for copy in copies_f + all_rims:
+
+    for n in far_first:
+        copies_r[n].wait_send()
+    for copy in copies:
         copy.wait_send()
 
 

time: 33.5 us -> 33 us (0.985)
  Pallas kernels: 32.8 us -> 32.2 us
    pallas_call x1, Pallas kernels: 32.1 us -> 31.5 us  [body(): pl.pallas_call(functools.partial(kernel, n_gx, n_gy), out_shape=(vmem(pop...]
where the time goes in v3:
time: 33 us; the launch traced here: 32.9 us
  Pallas kernels  32.2 us (98%)
  between operations  0.64 us (2%)
    pallas_call x1, Pallas kernels, body(): pl.pallas_call(functools.partial(kernel, n_gx, n_gy), out_shape=(vmem(pop...  31.5 us
    pallas_call x1, Pallas kernels, body(): pl.pallas_call(deliver, out_shape=(jax.ShapeDtypeStruct(populations.shape...  0.74 us

profile of v3, /device:TPU:1, one launch (start us, length us, event | category | flops | bytes accessed | tf_op | source)
XLA Modules:
  0.0 32.9 jit_solution(13461636914139507323)
XLA Ops:
  0.6 31.5 %shard_map.95 = (f32[19,4,8,128]{3,2,1,0:T(8,128)S(1)}, f32[3,16,128]{2,1,0:T(8,128)S(1)}) custom-call(f32[19,4,8,128]{3,2,1,0:T(8,128)} %pop_hbm.1, s32[4,8,128]{2,1,0:T(8,128)} %flags_hbm.1, s32[1,16]{1,0:T(1,128)} %bitcast.8, s32[16,128]{1,0:T(8,128)} %cell_hbm.1, f32[3,16,128]{2,1,0:T(8,128)} %bitcast.5, s32[16,128]{1,0:T(8,128)} %live_hbm.1, ...), custom_call_target="tpu_custom_call" | custom-call | tf_op jit(solution)/shard_map/pallas_call | solution.py:709
  32.1 0.7 %shard_map.96 = (f32[19,4,8,128]{3,2,1,0:T(8,128)}, f32[3,16,128]{2,1,0:T(8,128)}) custom-call(f32[19,4,8,128]{3,2,1,0:T(8,128)S(1)} %get-tuple-element.6.state, f32[3,16,128]{2,1,0:T(8,128)S(1)} %get-tuple-element.7.force), custom_call_target="tpu_custom_call" | custom-call | tf_op jit(solution)/shard_map/pallas_call | solution.py:766

commit v4 on v3

--- a/solution.py
+++ b/solution.py
@@ -197,7 +197,7 @@
     for n in far_first:
         pl.semaphore_signal(barrier, inc=1, device_id=device(near[n], 0), device_id_type=MESH)
     for dx, dy in NEIGHBOURS:
-        if dy != 0:
+        if dx == 0:
             pl.semaphore_signal(barrier, inc=1, device_id=device(dx, dy), device_id_type=MESH)
 
     in_pairs = (
@@ -302,13 +302,11 @@
         for number, (dx, dy) in enumerate(NEIGHBOURS)
     ]
 
-    pl.semaphore_wait(barrier, n_gx - 1 + 6)
+    pl.semaphore_wait(barrier, n_gx - 1 + 2)
     for n in far_first:
         copies_a[n].start()
     for n in far_first:
         copies_b[n].start()
-    for copy in copies_f:
-        copy.start()
 
     loads[6].wait()
 
@@ -570,6 +568,9 @@
                     build(n)
                 for n in members:
                     sample(n)
+        if step == 0:
+            for copy in copies_f:
+                copy.start()
         for members in groups:
             if step == 0:
                 for n in members:

time: 33 us -> 32.7 us (level)
  no operation moved by 1% of the time
where the time goes in v4:
time: 32.7 us; the launch traced here: 32.6 us
  Pallas kernels  32 us (98%)
  between operations  0.64 us (2%)
    pallas_call x1, Pallas kernels, body(): pl.pallas_call(functools.partial(kernel, n_gx, n_gy), out_shape=(vmem(pop...  31.2 us
    pallas_call x1, Pallas kernels, body(): pl.pallas_call(deliver, out_shape=(jax.ShapeDtypeStruct(populations.shape...  0.74 us

profile of v4, /device:TPU:1, one launch (start us, length us, event | category | flops | bytes accessed | tf_op | source)
XLA Modules:
  0.0 32.6 jit_solution(17346740859822557830)
XLA Ops:
  0.6 31.2 %shard_map.95 = (f32[19,4,8,128]{3,2,1,0:T(8,128)S(1)}, f32[3,16,128]{2,1,0:T(8,128)S(1)}) custom-call(f32[19,4,8,128]{3,2,1,0:T(8,128)} %pop_hbm.1, s32[4,8,128]{2,1,0:T(8,128)} %flags_hbm.1, s32[1,16]{1,0:T(1,128)} %bitcast.8, s32[16,128]{1,0:T(8,128)} %cell_hbm.1, f32[3,16,128]{2,1,0:T(8,128)} %bitcast.5, s32[16,128]{1,0:T(8,128)} %live_hbm.1, ...), custom_call_target="tpu_custom_call" | custom-call | tf_op jit(solution)/shard_map/pallas_call | solution.py:710
  31.9 0.7 %shard_map.96 = (f32[19,4,8,128]{3,2,1,0:T(8,128)}, f32[3,16,128]{2,1,0:T(8,128)}) custom-call(f32[19,4,8,128]{3,2,1,0:T(8,128)S(1)} %get-tuple-element.6.state, f32[3,16,128]{2,1,0:T(8,128)S(1)} %get-tuple-element.7.force), custom_call_target="tpu_custom_call" | custom-call | tf_op jit(solution)/shard_map/pallas_call | solution.py:767
